TPU v7x, 256 devices: a whole 4x4x8 slice. The times are simulated.
256 devices in a mesh: section: 8 (over y_lo, x), sc: 32 (over z, y_hi, core).
Axes of the slice: x: 4, y: 4 (y_hi: 2, y_lo: 2; y = y_hi * 2 + y_lo), z: 8, core: 2. Of those that a mesh axis runs over, the one named last changes fastest.
Arguments:
- observed_vector: float32 [4096, 14, 128], P('sc'), may hold values from -6 to 6
- propagation_matrix: float32 [4096, 16, 4, 128], P('sc', 'section'), may hold values from -0.5 to 0.5
- noise_var: float32 [4096], P('sc'), may hold values from 0.005 to 2.5, as said below
- sliced_constellation: int32 [4096, 14, 64], P('sc', None, 'section'), may hold values from 0 to 15
- detection_sequence: int32 [16], replicated, may hold values from 0 to 15, as said below
Outputs:
- estimates: float32 [4096, 14, 128], P('sc', None, 'section')
Inputs may be any that keep to these rules, and one draw needn't show every extreme that they name: `noise_var`: positive variances. `detection_sequence`: a permutation taken in blocks of 2 positions: each block of positions holds the 2 group ids 2 * m to 2 * m + 1 of one m, in a rotated order; the first block of positions takes m = 4, the second m = 0.
All inputs are finite; a program needn't handle non-finite values.
Results may differ from a plain program's by a relative error of at most 0.0001.
Values sent between devices are 32-bit elements; how exact they have to be, the bound alone decides.
No kernel may reach another device: no remote copies, remote signals or barrier semaphores. Data moves between devices by JAX's collectives and lax.ppermute only.
A program may use at most 64 MiB of HBM per device.

v0:
```python
import jax
import jax.numpy as jnp
from jax import lax
from jax.sharding import PartitionSpec as P

ROOT_TEN = 3.1622776601683795


def padded_2(value, sides, width):
    for axis, dim in sides:
        size, length = (lax.axis_size(axis), value.shape[dim])
        up = [(i, (i + 1) % size) for i in range(size - 1)]
        down = [(j, i) for i, j in up]
        last = lax.slice_in_dim(value, length - width, length, axis=dim)
        leading = lax.slice_in_dim(value, 0, width, axis=dim)
        before = lax.ppermute(last, axis, up)
        after = lax.ppermute(leading, axis, down)
        value = jnp.concatenate([before, value, after], axis=dim)
    return value


def sent_to_all(value, axis):
    copies = jnp.broadcast_to(value, (lax.axis_size(axis), *value.shape))
    return lax.all_to_all(copies, axis, split_axis=0, concat_axis=0, tiled=True)


def in_order(parts, dim):
    parts = jnp.moveaxis(parts, 0, dim)
    shape = parts.shape
    return parts.reshape(*shape[:dim], shape[dim] * shape[dim + 1], *shape[dim + 2 :])


def gather_directly(value, axis, dim):
    parts = sent_to_all(value, axis)
    return in_order(parts, dim)


def carried_in(part, axis, combine, identity):
    place = lax.axis_index(axis)
    gathered = lax.all_gather(part, axis)
    state = jnp.zeros_like(part) + jnp.asarray(identity, part.dtype)

    def one(step, state):
        return combine(state, lax.dynamic_index_in_dim(gathered, step, 0, False))

    return lax.fori_loop(0, place, one, state)


def over_copies(value, axis):
    everything = sent_to_all(value, axis)
    return jnp.sum(everything, axis=0)


def rotate(vectors):
    half = vectors.shape[-1] // 2
    return jnp.concatenate([-vectors[..., half:], vectors[..., :half]], axis=-1)


def symbol_values(constellation_labels):
    real_part = (2 * (constellation_labels % 4) - 3).astype(jnp.float32) / ROOT_TEN
    imag_part = (2 * (constellation_labels // 4) - 3).astype(jnp.float32) / ROOT_TEN
    return jnp.concatenate([real_part, imag_part], axis=-1)


def invert_small(gram):
    width = gram.shape[-1]
    entry = [[gram[..., i, j] for j in range(width)] for i in range(width)]
    lower = [[None] * width for i in range(width)]
    for j in range(width):
        pivot = entry[j][j]
        for k in range(j):
            pivot = pivot - lower[j][k] * lower[j][k]
        lower[j][j] = jnp.sqrt(pivot)
        recip = 1.0 / lower[j][j]
        for i in range(j + 1, width):
            value = entry[i][j]
            for k in range(j):
                value = value - lower[i][k] * lower[j][k]
            lower[i][j] = value * recip
    inv_lower = [[None] * width for i in range(width)]
    for i in range(width):
        inv_lower[i][i] = 1.0 / lower[i][i]
        for j in range(i):
            value = lower[i][j] * inv_lower[j][j]
            for k in range(j + 1, i):
                value = value + lower[i][k] * inv_lower[k][j]
            inv_lower[i][j] = -value * inv_lower[i][i]
    rows = []
    for i in range(width):
        cols = []
        for j in range(width):
            start = max(i, j)
            value = inv_lower[start][i] * inv_lower[start][j]
            for k in range(start + 1, width):
                value = value + inv_lower[k][i] * inv_lower[k][j]
            cols.append(value)
        rows.append(jnp.stack(cols, axis=-1))
    return jnp.stack(rows, axis=-2)


def filter_block(basis_all, noise):
    width = basis_all.shape[2]
    eye = jnp.eye(width, dtype=jnp.float32)
    gram = (
        jnp.einsum("sgik,sgjk->sgij", basis_all, basis_all, precision=lax.Precision.HIGHEST)
        + noise[:, None, None, None] * eye
    )
    inverse = invert_small(gram)
    filters = jnp.einsum("sgij,sgjk->sgik", inverse, basis_all, precision=lax.Precision.HIGHEST)
    diag = jnp.diagonal(inverse, axis1=2, axis2=3)[:, :, : width // 2]
    amplitude_level = 1.0 - noise[:, None, None] * diag
    return (filters, amplitude_level)


def local(observed_vector, propagation_matrix, noise_var, sliced_constellation, detection_sequence):
    blocks = propagation_matrix.shape[0]
    per_section = propagation_matrix.shape[1]
    users = propagation_matrix.shape[2]
    section_id = lax.axis_index("section")
    first = section_id * per_section
    padded = padded_2(propagation_matrix, (("sc", 0),), 1)
    smooth = 0.5 * padded[1:-1] + 0.25 * (padded[:-2] + padded[2:])
    basis_all = jnp.concatenate([smooth, rotate(smooth)], axis=2)
    every_code = gather_directly(sliced_constellation, "section", 2)
    group_count = every_code.shape[2] // users
    constellation_labels = jnp.take(
        every_code.reshape(blocks, every_code.shape[1], group_count, users),
        detection_sequence,
        axis=2,
    )
    symbols = symbol_values(constellation_labels)
    own_terms = []
    for slot in range(per_section):
        own_sym = lax.dynamic_index_in_dim(symbols, first + slot, 2, keepdims=False)
        own_terms.append(
            jnp.einsum("sti,sik->stk", own_sym, basis_all[:, slot], precision=lax.Precision.HIGHEST)
        )
    local_total = own_terms[0]
    for term in own_terms[1:]:
        local_total = local_total + term
    empty = jnp.zeros_like(observed_vector)
    earlier = carried_in(local_total, "section", lambda left, right: left + right, empty)
    current = observed_vector - earlier
    filters, amplitude_level = filter_block(basis_all, noise_var)
    totals = over_copies(jnp.sum(amplitude_level, axis=0), "sc")
    average_amplitude = totals / (blocks * lax.axis_size("sc"))
    results = []
    for slot in range(per_section):
        scale = jnp.concatenate([average_amplitude[slot], average_amplitude[slot]])
        est = (
            jnp.einsum("sik,stk->sti", filters[:, slot], current, precision=lax.Precision.HIGHEST)
            / scale
        )
        results.append(est)
        current = current - own_terms[slot]
    output = jnp.concatenate(results, axis=2)
    return output


def solution(mesh):
    in_specs = (
        P("sc", None, None),
        P("sc", "section", None, None),
        P("sc"),
        P("sc", None, "section"),
        P(),
    )
    out_specs = P("sc", None, "section")
    return jax.shard_map(local, mesh=mesh, in_specs=in_specs, out_specs=out_specs, check_vma=False)
```

profile of v0, /device:TPU:30, one launch (start us, length us, event | category | flops | bytes accessed | tf_op | source)
XLA Modules:
  0.0 157.2 jit_solution(17832464247681554382)
XLA Ops:
  7.2 1.9 %collective-permute-start = (f32[1,2,4,128]{3,2,1,0:T(4,128)S(1)}, f32[1,2,4,128]{3,2,1,0:T(4,128)S(1)}, u32[]{:S(2)}, u32[]{:S(2)}) collective-permute-start(f32[1,2,4,128]{3,2,1,0:T(4,128)S(1)} %get-tuple-element.182), channel_id=1, source_target_pairs={{0,1},{1,2},{2,3},{3,4},{4,5},{5,6},{6,7},{7,8},{8,9},{9,10},{10,1... | collective-permute-start | bytes 12296 | tf_op jit(solution)/shard_map/ppermute | solution.py:16
  9.2 5.1 %collective-permute-start.1 = (f32[1,2,4,128]{3,2,1,0:T(4,128)S(1)}, f32[1,2,4,128]{3,2,1,0:T(4,128)S(1)}, u32[]{:S(2)}, u32[]{:S(2)}) collective-permute-start(f32[1,2,4,128]{3,2,1,0:T(4,128)S(1)} %get-tuple-element.183), channel_id=1, source_target_pairs={{1,0},{2,1},{3,2},{4,3},{5,4},{6,5},{7,6},{8,7},{9,8},{10,9},{11,1... | collective-permute-start | bytes 12296 | tf_op jit(solution)/shard_map/ppermute | solution.py:17
  14.3 1.6 %broadcast_in_dim.32 = s32[8,128,14,8]{1,3,2,0:T(8,128)} broadcast(s32[128,14,8]{0,2,1:T(8,128)} %param.10), dimensions={1,2,3} | broadcast | bytes 516096 | tf_op jit(solution)/shard_map/broadcast_in_dim | solution.py:23
  15.9 5.7 %all-to-all-start = ((s32[8,128,14,8]{1,3,2,0:T(8,128)}), s32[8,128,14,8]{1,3,2,0:T(8,128)S(1)}, u32[]{:S(2)}, u32[]{:S(2)}) async-start(s32[8,128,14,8]{1,3,2,0:T(8,128)} %broadcast_in_dim.32), calls=%async_computation | async-start | bytes 917504 | tf_op jit(solution)/shard_map/all_to_all | solution.py:24
  23.0 1.9 %fusion.4 = f32[128,2,4,128]{3,2,1,0:T(4,128)S(1)} fusion(f32[1,2,4,128]{3,2,1,0:T(4,128)S(1)} %collective-permute-done.1, f32[128,2,4,128]{3,2,1,0:T(4,128)} %param.8, f32[1,2,4,128]{3,2,1,0:T(4,128)S(1)} %collective-permute-done), kind=kLoop, calls=%fused_computation.28 | loop fusion | flops 786432 | bytes 1056768 | tf_op jit(solution)/shard_map/add | solution.py:122
  25.6 2.4 %all-to-all-done = s32[8,128,14,8]{1,3,2,0:T(8,128)S(1)} async-done(((s32[8,128,14,8]{1,3,2,0:T(8,128)}), s32[8,128,14,8]{1,3,2,0:T(8,128)S(1)}, u32[]{:S(2)}, u32[]{:S(2)}) %all-to-all-start) | async-done | bytes 458784 | tf_op jit(solution)/shard_map/all_to_all | solution.py:24
  28.9 1.1 fusion.14
  30.6 1.8 %fusion.1 = f32[128,14,128]{2,1,0:T(8,128)S(1)} fusion(f32[128,2,8,128]{3,2,1,0:T(8,128)S(1)} %maximum_maximum_fusion, f32[128,14,1,8]{1,3,0,2:T(8,128)S(1)} %copy.2422), kind=kOutput, calls=%fused_computation.23 | convolution fusion | flops 22020096 | bytes 1966080 | tf_op jit(solution)/shard_map/sti,sik->stk/dot_general | solution.py:136
  32.5 1.8 %convolution_add_fusion.1 = f32[128,14,128]{2,1,0:T(8,128)S(1)} fusion(f32[128,14,128]{2,1,0:T(8,128)S(1)} %fusion.1, f32[128,2,8,128]{3,2,1,0:T(8,128)S(1)} %maximum_maximum_fusion, f32[128,14,1,8]{1,3,0,2:T(8,128)S(1)} %copy.2423), kind=kOutput, calls=%fused_computation.4 | convolution fusion | flops 22249472 | bytes 3014656 | tf_op jit(solution)/shard_map/sti,sik->stk/dot_general | solution.py:136
  34.3 1.2 copy.2424
  35.8 1.8 %convolution_add_fusion = f32[128,2,8,8]{3,2,1,0:T(8,128)S(1)} fusion(f32[128,2,8,128]{3,2,1,0:T(8,128)S(1)} %maximum_maximum_fusion, f32[128,8,8]{2,1,0:T(8,128)S(1)} %broadcast_multiply_fusion), kind=kOutput, calls=%fused_computation.3 | convolution fusion | flops 25182208 | bytes 1146880 | tf_op jit(solution)/shard_map/sgik,sgjk->sgij/dot_general | solution.py:105
  37.6 6.0 %fusion.173 = (f32[128,2,1,1]{3,2,1,0:T(1,128)S(1)}, f32[128,2,1,1]{3,2,1,0:T(1,128)}, f32[128,2,1,1]{3,2,1,0:T(1,128)}, f32[128,2,1,1]{3,2,1,0:T(1,128)}, f32[1...) fusion(f32[128,2,8,8]{3,2,1,0:T(8,128)S(1)} %convolution_add_fusion), kind=kLoop, calls=%fused_computation.335 | loop fusion | bytes 38912 | tf_op jit(solution)/shard_map/slice | solution.py:67
  43.7 4.5 %fusion.174 = (f32[128,2,1,1]{3,2,1,0:T(1,128)S(1)}, f32[128,2,1,1]{3,2,1,0:T(1,128)S(1)}, f32[128,2,1,1]{3,2,1,0:T(1,128)}, f32[128,2,1,1]{3,2,1,0:T(1,128)}, f...) fusion(f32[128,2,8,8]{3,2,1,0:T(8,128)S(1)} %convolution_add_fusion), kind=kLoop, calls=%fused_computation.336 | loop fusion | bytes 34816 | tf_op jit(solution)/shard_map/slice | solution.py:67
  49.2 1.0 copy.2438
  50.2 1.0 copy.2444
  51.2 1.0 copy.2451
  52.2 1.0 copy.2499
  54.2 1.0 copy.2456
  56.2 1.0 copy.2458
  59.2 1.0 copy.2464
  61.1 1.0 copy.2466
  64.1 1.0 copy.2472
  66.1 1.0 copy.2474
  68.1 1.0 copy.2476
  69.1 1.0 copy.2477
  70.2 1.0 copy.2437
  71.1 1.0 copy.2441
  73.1 1.0 copy.2443
  74.1 1.0 copy.2447
  76.1 1.0 copy.2449
  78.1 1.0 copy.2454
  84.6 2.8 %stack.50 = f32[128,2,8,8]{3,2,1,0:T(8,128)S(1)} concatenate(f32[128,2,1,8]{3,2,1,0:T(1,128)S(1)} %copy.2486, f32[128,2,1,8]{3,2,1,0:T(1,128)S(1)} %copy.2487, f32[128,2,1,8]{3,2,1,0:T(1,128)S(1)} %copy.2488, f32[128,2,1,8]{3,2,1,0:T(1,128)} %copy.2489, f32[128,2,1,8]{3,2,1,0:T(1,128)} %copy.2490, f32[128,2,1,8]{3,2,1,0:T(1,128)} %copy.2491, f32[128,2,1,8]{3,2,1,0:T(1,128)} %copy.2492, ...), dimensions={2} | concatenate | bytes 131072 | tf_op jit(solution)/shard_map/stack | solution.py:98
  89.2 11.3 %all-to-all-start.1 = ((f32[32,2,4]{2,1,0:T(2,128)}), f32[32,2,4]{2,1,0:T(2,128)S(1)}, u32[]{:S(2)}, u32[]{:S(2)}) async-start(f32[32,2,4]{2,1,0:T(2,128)} %broadcast_in_dim.35), calls=%async_computation.1 | async-start | bytes 65536 | tf_op jit(solution)/shard_map/all_to_all | solution.py:24
  100.5 2.8 %fusion.176 = f32[128,2,8,128]{3,2,1,0:T(8,128)} fusion(f32[128,2,8,8]{3,2,1,0:T(8,128)S(1)} %stack.50, f32[128,2,8,128]{3,2,1,0:T(8,128)S(1)} %maximum_maximum_fusion), kind=kOutput, calls=%fused_computation.338 | convolution fusion | flops 25165824 | bytes 2162688 | tf_op jit(solution)/shard_map/sgij,sgjk->sgik/dot_general | solution.py:109
  103.3 4.7 %all-to-all-done.1 = f32[32,2,4]{2,1,0:T(2,128)S(1)} async-done(((f32[32,2,4]{2,1,0:T(2,128)}), f32[32,2,4]{2,1,0:T(2,128)S(1)}, u32[]{:S(2)}, u32[]{:S(2)}) %all-to-all-start.1) | async-done | bytes 1056 | tf_op jit(solution)/shard_map/all_to_all | solution.py:24
  108.2 11.8 %all-gather.3.cloned.1.call-done = f32[1024,14,128]{2,0,1:T(8,128)} async-done(((f32[128,14,128]{2,0,1:T(8,128)}), f32[1024,14,128]{2,0,1:T(8,128)}) %all-gather.3.cloned.1.call-update) | async-done | bytes 7340048 | tf_op jit(solution)/shard_map/all_gather | solution.py:40
  120.0 10.7 %copy.2425 = f32[1024,14,128]{2,1,0:T(8,128)} copy(f32[1024,14,128]{2,0,1:T(8,128)} %all-gather.3.cloned.1.call-done) | data formatting | bytes 14680064 | tf_op jit(solution)/shard_map/all_gather | solution.py:40
  130.8 10.4 %while.10 = (s32[]{:T(128)}, f32[128,14,128]{2,1,0:T(8,128)S(1)}, s32[]{:T(128)}, f32[8,128,14,128]{3,2,1,0:T(8,128)}, s32[]{:T(128)}, /*index=5*/s32[]{:T(128)}, s32[]{:T(128)}) while((s32[]{:T(128)}, f32[128,14,128]{2,1,0:T(8,128)S(1)}, s32[]{:T(128)}, f32[8,128,14,128]{3,2,1,0:T(8,128)}, s32[]{:T(128)}, /*index=5*/s32[]{:T(128)}, ...), condition=%wide.region_1.2_spmd, body=%wide.region_0.1_spmd.sunk | while | flops 229381 | bytes 2752627 | solution.py:46
  130.8 1.5 bitcast_add_fusion.2
  132.4 1.5 bitcast_add_fusion.2
  133.8 1.5 bitcast_add_fusion.2
  135.3 1.5 bitcast_add_fusion.2
  136.8 1.5 bitcast_add_fusion.2
  138.3 1.5 bitcast_add_fusion.2
  139.8 1.5 bitcast_add_fusion.2
  141.2 3.2 %convolution_divide_fusion.1 = f32[128,14,8]{1,2,0:T(8,128)S(1)} fusion(f32[128,2,8,128]{3,2,1,0:T(8,128)} %fusion.176, f32[128,14,128]{2,1,0:T(8,128)S(1)} %get-tuple-element.28, f32[128,14,128]{2,0,1:T(8,128)S(1)} %copy-done, f32[8]{0:T(128)S(1)} %pad_maximum_fusion.3), kind=kOutput, calls=%fused_computation.6 | convolution fusion | flops 22263808 | bytes 2416672 | tf_op jit(solution)/shard_map/sik,stk->sti/dot_general | solution.py:151
  145.3 3.3 %convolution_divide_fusion = f32[128,14,8]{1,2,0:T(8,128)S(1)} fusion(f32[128,14,128]{2,1,0:T(8,128)S(1)} %fusion.1, f32[128,2,8,128]{3,2,1,0:T(8,128)} %fusion.176, f32[128,14,128]{2,1,0:T(8,128)S(1)} %get-tuple-element.28, f32[128,14,128]{2,0,1:T(8,128)S(1)} %copy-done, f32[8]{0:T(128)S(1)} %pad_maximum_fusion.4), kind=kOutput, calls=%fused_computation.5 | convolution fusion | flops 22493184 | bytes 3334176 | tf_op jit(solution)/shard_map/sik,stk->sti/dot_general | solution.py:151
  148.8 1.5 pad_maximum_fusion.2
  (102 shorter events, 26.1 us)
Async XLA Ops:
  7.2 15.7 %collective-permute-start = (f32[1,2,4,128]{3,2,1,0:T(4,128)S(1)}, f32[1,2,4,128]{3,2,1,0:T(4,128)S(1)}, u32[]{:S(2)}, u32[]{:S(2)}) collective-permute-start(f32[1,2,4,128]{3,2,1,0:T(4,128)S(1)} %get-tuple-element.182), channel_id=1, source_target_pairs={{0,1},{1,2},{2,3},{3,4},{4,5},{5,6},{6,7},{7,8},{8,9},{9,10},{10,1... | collective-permute-start | bytes 12296 | tf_op jit(solution)/shard_map/ppermute | solution.py:16
  9.2 13.8 %collective-permute-start.1 = (f32[1,2,4,128]{3,2,1,0:T(4,128)S(1)}, f32[1,2,4,128]{3,2,1,0:T(4,128)S(1)}, u32[]{:S(2)}, u32[]{:S(2)}) collective-permute-start(f32[1,2,4,128]{3,2,1,0:T(4,128)S(1)} %get-tuple-element.183), channel_id=1, source_target_pairs={{1,0},{2,1},{3,2},{4,3},{5,4},{6,5},{7,6},{8,7},{9,8},{10,9},{11,1... | collective-permute-start | bytes 12296 | tf_op jit(solution)/shard_map/ppermute | solution.py:17
  15.9 12.0 %all-to-all-start = ((s32[8,128,14,8]{1,3,2,0:T(8,128)}), s32[8,128,14,8]{1,3,2,0:T(8,128)S(1)}, u32[]{:S(2)}, u32[]{:S(2)}) async-start(s32[8,128,14,8]{1,3,2,0:T(8,128)} %broadcast_in_dim.32), calls=%async_computation | async-start | bytes 917504 | tf_op jit(solution)/shard_map/all_to_all | solution.py:24
  21.6 98.4 %all-gather.3.cloned.1.call-start = ((), (), s32[]{:S(2)}) async-start(), calls=%async_computation.2 | async-start | bytes 8257536 | tf_op jit(solution)/shard_map/all_gather | solution.py:40
  28.9 6.7 %copy-start.1 = (f32[128]{0:T(128)S(1)}, f32[128]{0:T(128)}, u32[]{:S(2)}) copy-start(f32[128]{0:T(128)} %param.9) | copy-start | bytes 1540
  89.2 18.8 %all-to-all-start.1 = ((f32[32,2,4]{2,1,0:T(2,128)}), f32[32,2,4]{2,1,0:T(2,128)S(1)}, u32[]{:S(2)}, u32[]{:S(2)}) async-start(f32[32,2,4]{2,1,0:T(2,128)} %broadcast_in_dim.35), calls=%async_computation.1 | async-start | bytes 65536 | tf_op jit(solution)/shard_map/all_to_all | solution.py:24
  130.7 10.5 %copy-start = (f32[128,14,128]{2,0,1:T(8,128)S(1)}, f32[128,14,128]{2,0,1:T(8,128)}, u32[]{:S(2)}) copy-start(f32[128,14,128]{2,0,1:T(8,128)} %param.7) | copy-start | bytes 2752516
Sparse Core Ops, SparseCore 0:
  35.7 84.3 all-gather.2
where the time goes:
time: 159 us; the launch traced here: 157 us
  local copies, waits for them, and re-layouts  67.6 us (43%)
  starting transfers between devices  24 us (15%)
  waiting for transfers between devices  18.9 us (12%)
  other arithmetic  17.9 us (11%)
  matrix products  14.7 us (9%)
  between operations  13.8 us (9%)
    slice x33, local copies, waits for them, and re-layouts, invert_small(): entry = [[gram[..., i, j] for j in range(width)] for i in range(width)]  38.5 us
    all_to_all x2, starting transfers between devices, sent_to_all(): return lax.all_to_all(copies, axis, split_axis=0, concat_axis=0, tiled=True)  17 us
    all_gather x1, waiting for transfers between devices, carried_in(): gathered = lax.all_gather(part, axis)  11.8 us
    all_gather x1, local copies, waits for them, and re-layouts, carried_in(): gathered = lax.all_gather(part, axis)  10.7 us
    add x7, other arithmetic, local(): left + right  10.2 us
    another operation x10, local copies, waits for them, and re-layouts, invert_small(): return jnp.stack(rows, axis=-2)  7.64 us
    all_to_all x2, waiting for transfers between devices, sent_to_all(): return lax.all_to_all(copies, axis, split_axis=0, concat_axis=0, tiled=True)  7.09 us
    dot_general x2, matrix products, local(): jnp.einsum('sik,stk->sti', filters[:, slot], current, precision=lax.Preci...  6.52 us
  transfers between devices with their start and end apart: 5, of which 3 were waited for; matrix products, arithmetic and copies ran while one was open for 39% of the time, Pallas kernels for 0%

commit v1 on v0

v1 whole, which is shorter than its diff:
```python
import jax
import jax.numpy as jnp
from jax import lax
from jax.experimental import pallas as pl
from jax.experimental.pallas import tpu as pltpu
from jax.sharding import PartitionSpec as P

ROOT_TEN = 3.1622776601683795
F32 = jnp.float32
BF16 = jnp.bfloat16
VMEM = pl.BlockSpec(memory_space=pltpu.VMEM)
PARAMS = pltpu.CompilerParams(vmem_limit_bytes=32 * 1024 * 1024)


def hermitian_inverse(a, b, noise):
    n = 4
    zr = [[None] * n for _ in range(n)]
    zi = [[None] * n for _ in range(n)]
    for i in range(n):
        for j in range(i + 1):
            zr[i][j] = a[j, i] + noise if i == j else a[j, i]
            zi[i][j] = None if i == j else b[j, i]
    lr = [[None] * n for _ in range(n)]
    li = [[None] * n for _ in range(n)]
    recip = [None] * n
    for j in range(n):
        d = zr[j][j]
        for k in range(j):
            d = d - (zr[j][k] * lr[j][k] + zi[j][k] * li[j][k])
        recip[j] = 1.0 / d
        for i in range(j + 1, n):
            re, im = zr[i][j], zi[i][j]
            for k in range(j):
                re = re - (zr[i][k] * lr[j][k] + zi[i][k] * li[j][k])
                im = im - (zi[i][k] * lr[j][k] - zr[i][k] * li[j][k])
            zr[i][j], zi[i][j] = re, im
            lr[i][j], li[i][j] = re * recip[j], im * recip[j]
    mr = [[None] * n for _ in range(n)]
    mi = [[None] * n for _ in range(n)]
    for j in range(n):
        for i in range(j + 1, n):
            re, im = lr[i][j], li[i][j]
            for k in range(j + 1, i):
                re = re + (lr[i][k] * mr[k][j] - li[i][k] * mi[k][j])
                im = im + (lr[i][k] * mi[k][j] + li[i][k] * mr[k][j])
            mr[i][j], mi[i][j] = -re, -im
    p, q = {}, {}
    for i in range(n):
        for j in range(i, n):
            if i == j:
                re, im = recip[j], None
            else:
                re, im = mr[j][i] * recip[j], -(mi[j][i] * recip[j])
            for k in range(j + 1, n):
                sr, si = mr[k][j] * recip[k], mi[k][j] * recip[k]
                re = re + (mr[k][i] * sr + mi[k][i] * si)
                if i != j:
                    im = im + (mr[k][i] * si - mi[k][i] * sr)
            p[i, j] = re
            if i != j:
                q[i, j] = im
    return p, q


def gram_entries(t_ref):
    a, b = {}, {}
    for g in range(2):
        sa, sb = {}, {}
        for c in range(8):
            x = [t_ref[g * 4 + u, c * 8 : c * 8 + 8, :] for u in range(4)]
            y = [t_ref[g * 4 + u, 64 + c * 8 : 72 + c * 8, :] for u in range(4)]
            for u in range(4):
                for w in range(u, 4):
                    v = x[u] * x[w] + y[u] * y[w]
                    sa[u, w] = v if c == 0 else sa[u, w] + v
                    if w > u:
                        v = y[u] * x[w] - x[u] * y[w]
                        sb[u, w] = v if c == 0 else sb[u, w] + v
        for key in sa:
            a.setdefault(key, []).append(jnp.sum(sa[key], axis=0, keepdims=True))
        for key in sb:
            b.setdefault(key, []).append(jnp.sum(sb[key], axis=0, keepdims=True))
    a = {key: jnp.concatenate(a[key], axis=0) for key in a}
    b = {key: jnp.concatenate(b[key], axis=0) for key in b}
    return a, b


def smooth_kernel(h_ref, before_ref, after_ref, labels_ref, x_ref):
    rows = 128
    for f in range(rows):
        left = before_ref[0] if f == 0 else h_ref[f - 1]
        right = after_ref[0] if f == rows - 1 else h_ref[f + 1]
        m, at = divmod(f, 16)
        x_ref[m, at * 8 : at * 8 + 8, :] = 0.5 * h_ref[f] + 0.25 * (left + right)
    labels = labels_ref[...].astype(F32)
    labels = jnp.concatenate([labels, jnp.zeros((16, 128), F32)], axis=0).T
    for m in range(8):
        x_ref[m, 128:144, :] = labels[m * 16 : m * 16 + 16, :]


def gain_kernel(x_ref, noise_ref, out_ref, t_ref):
    for i in range(8):
        rows = [x_ref[m, pl.ds(i, 16, stride=8), :] for m in range(8)]
        t_ref[i] = jnp.concatenate(rows, axis=0).T
    a, b = gram_entries(t_ref)
    noise = noise_ref[...]
    p, _ = hermitian_inverse(a, b, noise)
    out_ref[...] = jnp.concatenate([1.0 - noise * p[u, u] for u in range(4)], axis=0)


def detect_kernel(seq_ref, x_ref, y_ref, noise_ref, out_ref, ys_ref, yf_ref, v_ref, t_ref, f_ref, s_ref, e_ref, sem):
    me = lax.axis_index("section")
    first = pl.multiple_of(me * 16, 16)
    copy = pltpu.make_async_copy(y_ref.at[:, pl.ds(first, 16), :], ys_ref.at[pl.ds(0, 14)], sem)
    copy.start()
    ys_ref[14:16] = jnp.zeros((2, 16, 128), F32)

    for i in range(8):
        for f in range(16):
            v_ref[i, f * 8 : f * 8 + 8, :] = x_ref[pl.ds(f * 8 + i, 8, stride=144), :]
    for i in range(8):
        t_ref[i] = v_ref[i].T
    a, b = gram_entries(t_ref)
    column = jnp.broadcast_to(noise_ref[...], (128, 128)).T
    sub = lax.broadcasted_iota(jnp.int32, (128, 128), 0)
    lane = lax.broadcasted_iota(jnp.int32, (128, 128), 1)
    noise = jnp.sum(jnp.where(sub == first + lane // 8, column, 0.0), axis=0, keepdims=True)
    p, q = hermitian_inverse(a, b, noise)

    for g in range(2):
        pb = {key: jnp.broadcast_to(p[key][g : g + 1], (8, 128)) for key in p}
        qb = {key: jnp.broadcast_to(q[key][g : g + 1], (8, 128)) for key in q}
        for c in range(8):
            x = [t_ref[g * 4 + u, c * 8 : c * 8 + 8, :] for u in range(4)]
            y = [t_ref[g * 4 + u, 64 + c * 8 : 72 + c * 8, :] for u in range(4)]
            for u in range(4):
                fx = pb[u, u] * x[u]
                fy = pb[u, u] * y[u]
                for w in range(4):
                    if w != u:
                        key = (min(u, w), max(u, w))
                        fx = fx + pb[key] * x[w]
                        fy = fy + pb[key] * y[w]
                        if u < w:
                            fx = fx + qb[key] * y[w]
                            fy = fy - qb[key] * x[w]
                        else:
                            fx = fx - qb[key] * y[w]
                            fy = fy + qb[key] * x[w]
                f_ref[g * 4 + u, c * 8 : c * 8 + 8, :] = fx
                f_ref[g * 4 + u, 64 + c * 8 : 72 + c * 8, :] = fy
    for i in range(8):
        t_ref[i] = f_ref[i].T

    lane_row = lax.broadcasted_iota(jnp.int32, (1, 128), 1)
    lane_s, lane_u, lane_g = lane_row % 8, (lane_row // 8) % 4, (lane_row // 32) % 2
    wanted = jnp.zeros((1, 128), jnp.int32)
    for pos in range(16):
        wanted = jnp.where(lane_s * 2 + lane_g == pos, seq_ref[pos], wanted)
    row_u, row_g = sub % 4, (sub // 4) % 2
    own = lane[:16] // 8 == lax.broadcasted_iota(jnp.int32, (16, 128), 0)
    total = jnp.zeros((256, 128), F32)
    for m in range(8):
        pick = jnp.where((wanted == 2 * m + row_g) & (lane_u == row_u), 1.0, 0.0).astype(BF16)
        rows = []
        for f in range(16):
            at = m * 144 + 128 + f
            row = jnp.broadcast_to(x_ref[at : at + 1, :], (16, 128))
            rows.append(jnp.where(own, row, 0.0).astype(BF16))
        total = total + jnp.dot(jnp.concatenate(rows, axis=0), pick, preferred_element_type=F32)
    upper = jnp.floor(total * 0.25)
    re = 2.0 * (total - 4.0 * upper) - 3.0
    im = 2.0 * upper - 3.0
    for f in range(16):
        s_ref[f * 32 : f * 32 + 16, :] = re[f * 16 : f * 16 + 16]
        s_ref[f * 32 + 16 : f * 32 + 32, :] = im[f * 16 : f * 16 + 16]

    row = lax.broadcasted_iota(jnp.int32, (64, 128), 0)
    col = lax.broadcasted_iota(jnp.int32, (64, 128), 1)
    earlier = 2 * (row % 8) + row // 32 < 2 * (col % 8) + (col // 32) % 2
    sign = jnp.where(lane_row < 64, -1.0, 1.0)
    copy.wait()
    yf_ref[...] = ys_ref[...].reshape(256, 128)
    nt = (((1,), (1,)), ((), ()))
    for f in range(16):
        at = slice(f * 8, f * 8 + 8)
        filt = jnp.concatenate([t_ref[i, at, :] for i in range(8)], axis=0)
        filt = jnp.concatenate([filt, pltpu.roll(filt, 64, 1) * sign], axis=0)
        fh = filt.astype(BF16)
        fl = (filt - fh.astype(F32)).astype(BF16)
        left = jnp.concatenate([v_ref[i, at, :] for i in range(8)] + [yf_ref[pl.ds(f, 16, stride=16), :]], axis=0)
        lh = left.astype(BF16)
        ll = (left - lh.astype(F32)).astype(BF16)
        xz = lax.dot_general(lh, fh, nt, preferred_element_type=F32)
        xz = xz + lax.dot_general(lh, fl, nt, preferred_element_type=F32)
        xz = xz + lax.dot_general(ll, fh, nt, preferred_element_type=F32)
        cross = jnp.where(earlier, xz[:64], 0.0)
        ch = cross.astype(BF16)
        cl = (cross - ch.astype(F32)).astype(BF16)
        sym = s_ref[f * 32 : f * 32 + 32, :64].astype(BF16)
        gone = jnp.dot(sym, ch, preferred_element_type=F32) + jnp.dot(sym, cl, preferred_element_type=F32)
        gone = gone[:16] + pltpu.roll(gone[16:], 64, 1) * sign
        e_ref[pl.ds(f, 16, stride=16), :] = xz[64:] - gone * (1.0 / ROOT_TEN)

    for half in range(2):
        turned = e_ref[half * 128 : half * 128 + 128, :].T
        for c in range(2):
            for g in range(2):
                for u in range(4):
                    at = (c * 8 + g * 4 + u) * 8
                    out_ref[pl.ds(half * 16 + g * 8 + c * 4 + u, 8, stride=32), :] = turned[at : at + 8, :]


def finish_kernel(count, est_ref, gain_ref, out_ref):
    total = jnp.sum(gain_ref[...], axis=1, keepdims=True)
    recip = count / total
    block = lax.broadcasted_iota(jnp.int32, (8, 128), 1) // 16
    for g in range(2):
        users = [recip[u * 2 + g : u * 2 + g + 1] for u in range(4)]
        scale = jnp.broadcast_to(jnp.concatenate(users + users, axis=0), (8, 128))
        for half in range(2):
            x = [est_ref[m, half, g * 8 : g * 8 + 8, :] for m in range(8)]
            for bit in (1, 2, 4):
                low = (block & bit) == 0
                new = list(x)
                for i in range(8):
                    if i & bit == 0:
                        j = i | bit
                        new[i] = jnp.where(low, x[i], pltpu.roll(x[j], 16 * bit, 1))
                        new[j] = jnp.where(low, pltpu.roll(x[i], 128 - 16 * bit, 1), x[j])
                x = new
            for i in range(8):
                t = half * 8 + i
                if t < 14:
                    out_ref[t, g * 8 : g * 8 + 8, :] = x[i] * scale


def halo(h):
    size = lax.axis_size("sc")
    up = [(i, i + 1) for i in range(size - 1)]
    down = [(j, i) for i, j in up]
    return lax.ppermute(h[-1:], "sc", up), lax.ppermute(h[:1], "sc", down)


def over_sections(x):
    return lax.all_to_all(x, "section", split_axis=0, concat_axis=0, tiled=True)


def over_subcarriers(x):
    size = lax.axis_size("sc")
    bit = 1
    while bit < size:
        x = x + lax.ppermute(x, "sc", [(i, i ^ bit) for i in range(size)])
        bit *= 2
    return x


def local(observed_vector, propagation_matrix, noise_var, sliced_constellation, detection_sequence):
    h = propagation_matrix.reshape(128, 8, 128)
    noise = noise_var.reshape(1, 128)
    labels = sliced_constellation.transpose(1, 2, 0).reshape(112, 128)
    y = observed_vector.transpose(1, 0, 2)
    before, after = halo(h)
    smooth = pl.pallas_call(
        smooth_kernel,
        out_shape=jax.ShapeDtypeStruct((8, 144, 128), F32),
        in_specs=[VMEM] * 4,
        out_specs=VMEM,
        compiler_params=PARAMS,
        name="smooth",
    )(h, before, after, labels)
    gathered = over_sections(smooth)
    gain = pl.pallas_call(
        gain_kernel,
        out_shape=jax.ShapeDtypeStruct((8, 128), F32),
        in_specs=[VMEM] * 2,
        out_specs=VMEM,
        scratch_shapes=[pltpu.VMEM((8, 128, 128), F32)],
        compiler_params=PARAMS,
        name="gain",
    )(smooth, noise)
    gain = over_subcarriers(gain)
    estimates = pl.pallas_call(
        detect_kernel,
        out_shape=jax.ShapeDtypeStruct((256, 128), F32),
        in_specs=[pl.BlockSpec(memory_space=pltpu.SMEM), VMEM, pl.BlockSpec(memory_space=pl.ANY), VMEM],
        out_specs=VMEM,
        scratch_shapes=[
            pltpu.VMEM((16, 16, 128), F32),
            pltpu.VMEM((256, 128), F32),
            pltpu.VMEM((8, 128, 128), F32),
            pltpu.VMEM((8, 128, 128), F32),
            pltpu.VMEM((8, 128, 128), F32),
            pltpu.VMEM((512, 128), F32),
            pltpu.VMEM((256, 128), F32),
            pltpu.SemaphoreType.DMA,
        ],
        compiler_params=PARAMS,
        name="detect",
    )(detection_sequence, gathered.reshape(1152, 128), y, noise)
    estimates = over_sections(estimates.reshape(8, 2, 16, 128))
    count = float(128 * lax.axis_size("sc"))
    out = pl.pallas_call(
        lambda *refs: finish_kernel(count, *refs),
        out_shape=jax.ShapeDtypeStruct((14, 16, 128), F32),
        in_specs=[VMEM] * 2,
        out_specs=VMEM,
        compiler_params=PARAMS,
        name="finish",
    )(estimates, gain)
    return out.transpose(2, 0, 1)


def solution(mesh):
    in_specs = (
        P("sc", None, None),
        P("sc", "section", None, None),
        P("sc"),
        P("sc", None, "section"),
        P(),
    )
    out_specs = P("sc", None, "section")
    return jax.shard_map(local, mesh=mesh, in_specs=in_specs, out_specs=out_specs, check_vma=False)
```

time: 159 us -> 64.4 us (0.41)
  the two profiles are of different devices: /device:TPU:30 before, /device:TPU:2 now
where the time goes in v1:
time: 64.4 us; the launch traced here: 64 us
  starting transfers between devices  29 us (45%)
  blocking collectives  13.2 us (20%)
  waiting for transfers between devices  11.9 us (18%)
  Pallas kernels  6.59 us (10%)
  local copies, waits for them, and re-layouts  3.24 us (5%)
    ppermute x5, starting transfers between devices, over_subcarriers(): x = x + lax.ppermute(x, 'sc', [(i, i ^ bit) for i in range(size)])  21 us
    all_to_all x1, blocking collectives, over_sections(): return lax.all_to_all(x, 'section', split_axis=0, concat_axis=0, tiled=True)  13.2 us
    ppermute x5, waiting for transfers between devices, over_subcarriers(): x = x + lax.ppermute(x, 'sc', [(i, i ^ bit) for i in range(size)])  7.16 us
    pallas_call x1, Pallas kernels, local(): pl.pallas_call(detect_kernel, out_shape=jax.ShapeDtypeStruct((256, 128),...  5.27 us
    all_to_all x1, starting transfers between devices, over_sections(): return lax.all_to_all(x, 'section', split_axis=0, concat_axis=0, tiled=True)  4.92 us
    ppermute x2, waiting for transfers between devices, halo(): return (lax.ppermute(h[-1:], 'sc', up), lax.ppermute(h[:1], 'sc', down))  4.73 us
    ppermute x2, starting transfers between devices, halo(): return (lax.ppermute(h[-1:], 'sc', up), lax.ppermute(h[:1], 'sc', down))  3.02 us
    unnamed x10, local copies, waits for them, and re-layouts  2.53 us
  transfers between devices with their start and end apart: 8, of which 6 were waited for; matrix products, arithmetic and copies ran while one was open for 0% of the time, Pallas kernels for 0%

profile of v1, /device:TPU:2, one launch (start us, length us, event | category | flops | bytes accessed | tf_op | source)
XLA Modules:
  0.0 64.0 jit_solution(10117882348396138123)
XLA Ops:
  0.0 0.7 %fusion = (f32[1,2,4,128]{3,2,1,0:T(4,128)S(1)}, f32[1,2,4,128]{3,2,1,0:T(4,128)S(1)}) fusion(f32[128,2,4,128]{3,2,1,0:T(4,128)} %param.6), kind=kLoop, calls=%fused_computation | loop fusion | bytes 16384 | tf_op jit(solution)/shard_map/slice | solution.py:242
  0.7 1.7 %collective-permute-start = (f32[1,8,128]{2,1,0:T(8,128)S(1)}, f32[1,8,128]{2,1,0:T(8,128)S(1)}, u32[]{:S(2)}, u32[]{:S(2)}) collective-permute-start(f32[1,8,128]{2,1,0:T(8,128)S(1)} %bitcast.18), channel_id=1, source_target_pairs={{0,1},{1,2},{2,3},{3,4},{4,5},{5,6},{6,7},{7,8},{8,9},{9,10},{10,1... | collective-permute-start | bytes 12296 | tf_op jit(solution)/shard_map/ppermute | solution.py:242
  2.4 1.3 %collective-permute-start.1 = (f32[1,8,128]{2,1,0:T(8,128)S(1)}, f32[1,8,128]{2,1,0:T(8,128)S(1)}, u32[]{:S(2)}, u32[]{:S(2)}) collective-permute-start(f32[1,8,128]{2,1,0:T(8,128)S(1)} %bitcast.17), channel_id=1, source_target_pairs={{1,0},{2,1},{3,2},{4,3},{5,4},{6,5},{7,6},{8,7},{9,8},{10,9},{11,1... | collective-permute-start | bytes 12296 | tf_op jit(solution)/shard_map/ppermute | solution.py:242
  3.7 0.0 collective-permute-done.before_ref
  3.8 4.7 %collective-permute-done.1.after_ref = f32[1,8,128]{2,1,0:T(8,128)S(1)} collective-permute-done((f32[1,8,128]{2,1,0:T(8,128)S(1)}, f32[1,8,128]{2,1,0:T(8,128)S(1)}, u32[]{:S(2)}, u32[]{:S(2)}) %collective-permute-start.1) | collective-permute-done | bytes 4128 | tf_op jit(solution)/shard_map/ppermute | solution.py:242
  8.5 0.0 copy-start.1
  8.5 1.0 %copy-done.1 = f32[128,2,4,128]{3,2,1,0:T(4,128)S(1)} copy-done((f32[128,2,4,128]{3,2,1,0:T(4,128)S(1)}, f32[128,2,4,128]{3,2,1,0:T(4,128)}, u32[]{:S(2)}) %copy-start.1) | copy-done | bytes 524312
  9.5 0.0 copy-start.2
  9.5 0.8 %copy-done.2 = s32[128,14,8]{0,2,1:T(8,128)S(1)} copy-done((s32[128,14,8]{0,2,1:T(8,128)S(1)}, s32[128,14,8]{0,2,1:T(8,128)}, u32[]{:S(2)}) %copy-start.2) | copy-done | bytes 57368
  10.3 0.0 copy-start
  10.3 0.1 smooth.1.x_ref
  10.4 13.2 %all_to_all.10 = f32[8,144,128]{2,1,0:T(8,128)S(1)} all-to-all(f32[8,144,128]{2,1,0:T(8,128)S(1)} %smooth.1.x_ref), channel_id=1, replica_groups=mesh['section'=8,'sc'=32] {'section'}, dimensions={0} | all-to-all | bytes 1179648 | tf_op jit(solution)/shard_map/all_to_all | solution.py:246
  23.7 0.0 copy-start.3
  23.7 0.0 copy-start.4
  23.7 0.0 copy-done
  23.7 0.6 %copy-done.3 = f32[128]{0:T(128)S(1)} copy-done((f32[128]{0:T(128)S(1)}, f32[128]{0:T(128)}, u32[]{:S(2)}) %copy-start.3) | copy-done | bytes 536
  24.3 0.0 copy-done.4
  24.3 5.3 %detect.1 = f32[256,128]{1,0:T(8,128)} custom-call(s32[16]{0:T(128)S(1)} %copy-done.4, f32[1152,128]{1,0:T(8,128)S(1)} %bitcast.11, f32[14,128,128]{2,1,0:T(8,128)S(1)} %bitcast.12, f32[1,128]{1,0:T(1,128)S(1)} %bitcast.15), custom_call_target="tpu_custom_call" | custom-call | tf_op jit(solution)/shard_map/detect/pallas_call | solution.py:283
  29.6 4.9 %all-to-all-start.1 = ((f32[8,2,16,128]{3,2,1,0:T(8,128)}), f32[8,2,16,128]{3,2,1,0:T(8,128)S(1)}, u32[]{:S(2)}, u32[]{:S(2)}) async-start(f32[8,2,16,128]{3,2,1,0:T(8,128)} %bitcast.8), calls=%async_computation.1 | async-start | bytes 262144 | tf_op jit(solution)/shard_map/all_to_all | solution.py:246
  34.5 0.3 gain.1
  34.9 2.0 %collective-permute-start.2 = (f32[8,128]{1,0:T(8,128)S(1)}, f32[8,128]{1,0:T(8,128)S(1)}, u32[]{:S(2)}, u32[]{:S(2)}) collective-permute-start(f32[8,128]{1,0:T(8,128)S(1)} %gain.1), channel_id=1, source_target_pairs={{0,1},{1,0},{2,3},{3,2},{4,5},{5,4},{6,7},{7,6},{8,9},{9,8},{10,11... | collective-permute-start | bytes 12296 | tf_op jit(solution)/shard_map/ppermute | solution.py:253
  36.8 0.8 %collective-permute-done.2 = f32[8,128]{1,0:T(8,128)S(1)} collective-permute-done((f32[8,128]{1,0:T(8,128)S(1)}, f32[8,128]{1,0:T(8,128)S(1)}, u32[]{:S(2)}, u32[]{:S(2)}) %collective-permute-start.2) | collective-permute-done | bytes 4128 | tf_op jit(solution)/shard_map/ppermute | solution.py:253
  37.6 4.4 %collective-permute-start.3 = (f32[8,128]{1,0:T(8,128)S(1)}, f32[8,128]{1,0:T(8,128)S(1)}, u32[]{:S(2)}, u32[]{:S(2)}) collective-permute-start(f32[8,128]{1,0:T(8,128)S(1)} %add.15), channel_id=1, source_target_pairs={{0,2},{1,3},{2,0},{3,1},{4,6},{5,7},{6,4},{7,5},{8,10},{9,11},{10,... | collective-permute-start | bytes 12296 | tf_op jit(solution)/shard_map/ppermute | solution.py:253
  42.0 1.6 %collective-permute-done.3 = f32[8,128]{1,0:T(8,128)S(1)} collective-permute-done((f32[8,128]{1,0:T(8,128)S(1)}, f32[8,128]{1,0:T(8,128)S(1)}, u32[]{:S(2)}, u32[]{:S(2)}) %collective-permute-start.3) | collective-permute-done | bytes 4128 | tf_op jit(solution)/shard_map/ppermute | solution.py:253
  43.6 3.9 %collective-permute-start.4 = (f32[8,128]{1,0:T(8,128)S(1)}, f32[8,128]{1,0:T(8,128)S(1)}, u32[]{:S(2)}, u32[]{:S(2)}) collective-permute-start(f32[8,128]{1,0:T(8,128)S(1)} %add.16), channel_id=1, source_target_pairs={{0,4},{1,5},{2,6},{3,7},{4,0},{5,1},{6,2},{7,3},{8,12},{9,13},{10,... | collective-permute-start | bytes 12296 | tf_op jit(solution)/shard_map/ppermute | solution.py:253
  47.5 1.6 %collective-permute-done.4 = f32[8,128]{1,0:T(8,128)S(1)} collective-permute-done((f32[8,128]{1,0:T(8,128)S(1)}, f32[8,128]{1,0:T(8,128)S(1)}, u32[]{:S(2)}, u32[]{:S(2)}) %collective-permute-start.4) | collective-permute-done | bytes 4128 | tf_op jit(solution)/shard_map/ppermute | solution.py:253
  49.1 3.4 %collective-permute-start.5 = (f32[8,128]{1,0:T(8,128)S(1)}, f32[8,128]{1,0:T(8,128)S(1)}, u32[]{:S(2)}, u32[]{:S(2)}) collective-permute-start(f32[8,128]{1,0:T(8,128)S(1)} %add.17), channel_id=1, source_target_pairs={{0,8},{1,9},{2,10},{3,11},{4,12},{5,13},{6,14},{7,15},{8,0},{9,1},... | collective-permute-start | bytes 12296 | tf_op jit(solution)/shard_map/ppermute | solution.py:253
  52.5 1.6 %collective-permute-done.5 = f32[8,128]{1,0:T(8,128)S(1)} collective-permute-done((f32[8,128]{1,0:T(8,128)S(1)}, f32[8,128]{1,0:T(8,128)S(1)}, u32[]{:S(2)}, u32[]{:S(2)}) %collective-permute-start.5) | collective-permute-done | bytes 4128 | tf_op jit(solution)/shard_map/ppermute | solution.py:253
  54.1 7.4 %collective-permute-start.6 = (f32[8,128]{1,0:T(8,128)S(1)}, f32[8,128]{1,0:T(8,128)S(1)}, u32[]{:S(2)}, u32[]{:S(2)}) collective-permute-start(f32[8,128]{1,0:T(8,128)S(1)} %add.18), channel_id=1, source_target_pairs={{0,16},{1,17},{2,18},{3,19},{4,20},{5,21},{6,22},{7,23},{8,24},{9,... | collective-permute-start | bytes 12296 | tf_op jit(solution)/shard_map/ppermute | solution.py:253
  61.5 1.6 %collective-permute-done.6 = f32[8,128]{1,0:T(8,128)S(1)} collective-permute-done((f32[8,128]{1,0:T(8,128)S(1)}, f32[8,128]{1,0:T(8,128)S(1)}, u32[]{:S(2)}, u32[]{:S(2)}) %collective-permute-start.6) | collective-permute-done | bytes 4128 | tf_op jit(solution)/shard_map/ppermute | solution.py:253
  63.1 0.0 all-to-all-done.1.refs_0_
  63.1 0.9 %finish.1 = f32[14,16,128]{2,1,0:T(8,128)} custom-call(f32[8,2,16,128]{3,2,1,0:T(8,128)S(1)} %all-to-all-done.1.refs_0_, f32[8,128]{1,0:T(8,128)S(1)} %add.19.refs_1_), custom_call_target="tpu_custom_call" | custom-call | tf_op jit(solution)/shard_map/finish/pallas_call | solution.py:303
  (5 shorter events, 0.0 us)
Async XLA Ops:
  0.7 3.0 %collective-permute-start = (f32[1,8,128]{2,1,0:T(8,128)S(1)}, f32[1,8,128]{2,1,0:T(8,128)S(1)}, u32[]{:S(2)}, u32[]{:S(2)}) collective-permute-start(f32[1,8,128]{2,1,0:T(8,128)S(1)} %bitcast.18), channel_id=1, source_target_pairs={{0,1},{1,2},{2,3},{3,4},{4,5},{5,6},{6,7},{7,8},{8,9},{9,10},{10,1... | collective-permute-start | bytes 12296 | tf_op jit(solution)/shard_map/ppermute | solution.py:242
  2.4 6.0 %collective-permute-start.1 = (f32[1,8,128]{2,1,0:T(8,128)S(1)}, f32[1,8,128]{2,1,0:T(8,128)S(1)}, u32[]{:S(2)}, u32[]{:S(2)}) collective-permute-start(f32[1,8,128]{2,1,0:T(8,128)S(1)} %bitcast.17), channel_id=1, source_target_pairs={{1,0},{2,1},{3,2},{4,3},{5,4},{6,5},{7,6},{8,7},{9,8},{10,9},{11,1... | collective-permute-start | bytes 12296 | tf_op jit(solution)/shard_map/ppermute | solution.py:242
  8.5 1.0 %copy-start.1 = (f32[128,2,4,128]{3,2,1,0:T(4,128)S(1)}, f32[128,2,4,128]{3,2,1,0:T(4,128)}, u32[]{:S(2)}) copy-start(f32[128,2,4,128]{3,2,1,0:T(4,128)} %param.6) | copy-start | bytes 1572868
  9.5 0.8 %copy-start.2 = (s32[128,14,8]{0,2,1:T(8,128)S(1)}, s32[128,14,8]{0,2,1:T(8,128)}, u32[]{:S(2)}) copy-start(s32[128,14,8]{0,2,1:T(8,128)} %param.8) | copy-start | bytes 172036
  10.3 13.3 %copy-start = (f32[128,14,128]{2,0,1:T(8,128)S(1)}, f32[128,14,128]{2,0,1:T(8,128)}, u32[]{:S(2)}) copy-start(f32[128,14,128]{2,0,1:T(8,128)} %param.5) | copy-start | bytes 2752516
  23.7 0.7 %copy-start.3 = (f32[128]{0:T(128)S(1)}, f32[128]{0:T(128)}, u32[]{:S(2)}) copy-start(f32[128]{0:T(128)} %param.7) | copy-start | bytes 1540
  23.7 0.7 %copy-start.4 = (s32[16]{0:T(128)S(1)}, s32[16]{0:T(128)}, u32[]{:S(2)}) copy-start(s32[16]{0:T(128)} %seq_ref.1) | copy-start | bytes 196
  29.6 33.5 %all-to-all-start.1 = ((f32[8,2,16,128]{3,2,1,0:T(8,128)}), f32[8,2,16,128]{3,2,1,0:T(8,128)S(1)}, u32[]{:S(2)}, u32[]{:S(2)}) async-start(f32[8,2,16,128]{3,2,1,0:T(8,128)} %bitcast.8), calls=%async_computation.1 | async-start | bytes 262144 | tf_op jit(solution)/shard_map/all_to_all | solution.py:246
  34.9 2.8 %collective-permute-start.2 = (f32[8,128]{1,0:T(8,128)S(1)}, f32[8,128]{1,0:T(8,128)S(1)}, u32[]{:S(2)}, u32[]{:S(2)}) collective-permute-start(f32[8,128]{1,0:T(8,128)S(1)} %gain.1), channel_id=1, source_target_pairs={{0,1},{1,0},{2,3},{3,2},{4,5},{5,4},{6,7},{7,6},{8,9},{9,8},{10,11... | collective-permute-start | bytes 12296 | tf_op jit(solution)/shard_map/ppermute | solution.py:253
  37.6 6.0 %collective-permute-start.3 = (f32[8,128]{1,0:T(8,128)S(1)}, f32[8,128]{1,0:T(8,128)S(1)}, u32[]{:S(2)}, u32[]{:S(2)}) collective-permute-start(f32[8,128]{1,0:T(8,128)S(1)} %add.15), channel_id=1, source_target_pairs={{0,2},{1,3},{2,0},{3,1},{4,6},{5,7},{6,4},{7,5},{8,10},{9,11},{10,... | collective-permute-start | bytes 12296 | tf_op jit(solution)/shard_map/ppermute | solution.py:253
  43.6 5.5 %collective-permute-start.4 = (f32[8,128]{1,0:T(8,128)S(1)}, f32[8,128]{1,0:T(8,128)S(1)}, u32[]{:S(2)}, u32[]{:S(2)}) collective-permute-start(f32[8,128]{1,0:T(8,128)S(1)} %add.16), channel_id=1, source_target_pairs={{0,4},{1,5},{2,6},{3,7},{4,0},{5,1},{6,2},{7,3},{8,12},{9,13},{10,... | collective-permute-start | bytes 12296 | tf_op jit(solution)/shard_map/ppermute | solution.py:253
  49.1 5.0 %collective-permute-start.5 = (f32[8,128]{1,0:T(8,128)S(1)}, f32[8,128]{1,0:T(8,128)S(1)}, u32[]{:S(2)}, u32[]{:S(2)}) collective-permute-start(f32[8,128]{1,0:T(8,128)S(1)} %add.17), channel_id=1, source_target_pairs={{0,8},{1,9},{2,10},{3,11},{4,12},{5,13},{6,14},{7,15},{8,0},{9,1},... | collective-permute-start | bytes 12296 | tf_op jit(solution)/shard_map/ppermute | solution.py:253
  54.1 9.0 %collective-permute-start.6 = (f32[8,128]{1,0:T(8,128)S(1)}, f32[8,128]{1,0:T(8,128)S(1)}, u32[]{:S(2)}, u32[]{:S(2)}) collective-permute-start(f32[8,128]{1,0:T(8,128)S(1)} %add.18), channel_id=1, source_target_pairs={{0,16},{1,17},{2,18},{3,19},{4,20},{5,21},{6,22},{7,23},{8,24},{9,... | collective-permute-start | bytes 12296 | tf_op jit(solution)/shard_map/ppermute | solution.py:253

commit v2 on v1

v2 whole, which is shorter than its diff:
```python
import jax
import jax.numpy as jnp
from jax import lax
from jax.experimental import pallas as pl
from jax.experimental.pallas import tpu as pltpu
from jax.sharding import PartitionSpec as P

ROOT_TEN = 3.1622776601683795
F32 = jnp.float32
BF16 = jnp.bfloat16
VMEM = pl.BlockSpec(memory_space=pltpu.VMEM)
ANY = pl.BlockSpec(memory_space=pl.ANY)
PARAMS = pltpu.CompilerParams(vmem_limit_bytes=32 * 1024 * 1024)


def hermitian_inverse(a, b, noise):
    n = 4
    zr = [[None] * n for _ in range(n)]
    zi = [[None] * n for _ in range(n)]
    for i in range(n):
        for j in range(i + 1):
            zr[i][j] = a[j, i] + noise if i == j else a[j, i]
            zi[i][j] = None if i == j else b[j, i]
    lr = [[None] * n for _ in range(n)]
    li = [[None] * n for _ in range(n)]
    recip = [None] * n
    for j in range(n):
        d = zr[j][j]
        for k in range(j):
            d = d - (zr[j][k] * lr[j][k] + zi[j][k] * li[j][k])
        recip[j] = 1.0 / d
        for i in range(j + 1, n):
            re, im = zr[i][j], zi[i][j]
            for k in range(j):
                re = re - (zr[i][k] * lr[j][k] + zi[i][k] * li[j][k])
                im = im - (zi[i][k] * lr[j][k] - zr[i][k] * li[j][k])
            zr[i][j], zi[i][j] = re, im
            lr[i][j], li[i][j] = re * recip[j], im * recip[j]
    mr = [[None] * n for _ in range(n)]
    mi = [[None] * n for _ in range(n)]
    for j in range(n):
        for i in range(j + 1, n):
            re, im = lr[i][j], li[i][j]
            for k in range(j + 1, i):
                re = re + (lr[i][k] * mr[k][j] - li[i][k] * mi[k][j])
                im = im + (lr[i][k] * mi[k][j] + li[i][k] * mr[k][j])
            mr[i][j], mi[i][j] = -re, -im
    p, q = {}, {}
    for i in range(n):
        for j in range(i, n):
            if i == j:
                re, im = recip[j], None
            else:
                re, im = mr[j][i] * recip[j], -(mi[j][i] * recip[j])
            for k in range(j + 1, n):
                sr, si = mr[k][j] * recip[k], mi[k][j] * recip[k]
                re = re + (mr[k][i] * sr + mi[k][i] * si)
                if i != j:
                    im = im + (mr[k][i] * si - mi[k][i] * sr)
            p[i, j] = re
            if i != j:
                q[i, j] = im
    return p, q


def gram_entries(t_ref):
    a, b = {}, {}
    for g in range(2):
        sa, sb = {}, {}
        for c in range(8):
            x = [t_ref[g * 4 + u, c * 8 : c * 8 + 8, :] for u in range(4)]
            y = [t_ref[g * 4 + u, 64 + c * 8 : 72 + c * 8, :] for u in range(4)]
            for u in range(4):
                for w in range(u, 4):
                    v = x[u] * x[w] + y[u] * y[w]
                    sa[u, w] = v if c == 0 else sa[u, w] + v
                    if w > u:
                        v = y[u] * x[w] - x[u] * y[w]
                        sb[u, w] = v if c == 0 else sb[u, w] + v
        for key in sa:
            a.setdefault(key, []).append(jnp.sum(sa[key], axis=0, keepdims=True))
        for key in sb:
            b.setdefault(key, []).append(jnp.sum(sb[key], axis=0, keepdims=True))
    a = {key: jnp.concatenate(a[key], axis=0) for key in a}
    b = {key: jnp.concatenate(b[key], axis=0) for key in b}
    return a, b


def inner_kernel(seq_ref, h_ref, labels_ref, noise_ref, x_ref, aux_ref):
    for f in range(128):
        m, at = divmod(f, 16)
        if 0 < f < 127:
            x_ref[m, at * 8 : at * 8 + 8, :] = 0.5 * h_ref[f] + 0.25 * (h_ref[f - 1] + h_ref[f + 1])
        else:
            near = h_ref[1] if f == 0 else h_ref[126]
            x_ref[m, at * 8 : at * 8 + 8, :] = 0.5 * h_ref[f] + 0.25 * near
    labels = labels_ref[...].astype(F32)
    labels = jnp.concatenate([labels, jnp.zeros((16, 128), F32)], axis=0).T
    for m in range(8):
        x_ref[m, 128:144, :] = labels[m * 16 : m * 16 + 16, :]
    noise = noise_ref[...]
    column = jnp.broadcast_to(noise, (128, 128)).T
    sub = lax.broadcasted_iota(jnp.int32, (128, 128), 0)
    lane = lax.broadcasted_iota(jnp.int32, (128, 128), 1)
    first = lax.axis_index("section") * 16
    spread = jnp.sum(jnp.where(sub == first + lane // 8, column, 0.0), axis=0, keepdims=True)
    position = 2 * (lane[:1] % 8) + (lane[:1] // 32) % 2
    wanted = jnp.zeros((1, 128), jnp.int32)
    for pos in range(16):
        wanted = jnp.where(position == pos, seq_ref[pos], wanted)
    aux_ref[...] = jnp.concatenate([noise, spread, wanted.astype(F32), jnp.zeros((5, 128), F32)], axis=0)


def edge_kernel(x_ref, close_ref, far_ref, out_ref):
    even = lax.axis_index("sc") % 2 == 0
    close, far = close_ref[0], far_ref[0]
    out_ref[...] = x_ref[...]
    out_ref[0, 0:8, :] = x_ref[0, 0:8, :] + 0.25 * jnp.where(even, far, close)
    out_ref[7, 120:128, :] = x_ref[7, 120:128, :] + 0.25 * jnp.where(even, close, far)


def add_kernel(x_ref, other_ref, order_ref, out_ref):
    out_ref[...] = x_ref[...] + other_ref[...]


def gain_kernel(x_ref, close_ref, far_ref, aux_ref, out_ref, t_ref):
    even = lax.axis_index("sc") % 2 == 0
    close, far = close_ref[0], far_ref[0]
    before = 0.25 * jnp.where(even, far, close)
    after = 0.25 * jnp.where(even, close, far)
    row = lax.broadcasted_iota(jnp.int32, (16, 128), 0)
    for i in range(8):
        rows = [x_ref[m, pl.ds(i, 16, stride=8), :] for m in range(8)]
        rows[0] = rows[0] + jnp.where(row == 0, before[i : i + 1], 0.0)
        rows[7] = rows[7] + jnp.where(row == 15, after[i : i + 1], 0.0)
        t_ref[i] = jnp.concatenate(rows, axis=0).T
    a, b = gram_entries(t_ref)
    noise = aux_ref[0:1]
    p, _ = hermitian_inverse(a, b, noise)
    out_ref[...] = jnp.concatenate([1.0 - noise * p[u, u] for u in range(4)], axis=0)


def filter_kernel(x_ref, aux_ref, order_ref, v_ref, w_ref, s_ref, t_ref, f_ref):
    for i in range(8):
        for f in range(16):
            v_ref[i, f * 8 : f * 8 + 8, :] = x_ref[pl.ds(f * 8 + i, 8, stride=144), :]
    for i in range(8):
        t_ref[i] = v_ref[i].T
    a, b = gram_entries(t_ref)
    p, q = hermitian_inverse(a, b, aux_ref[1:2])

    for g in range(2):
        pb = {key: jnp.broadcast_to(p[key][g : g + 1], (8, 128)) for key in p}
        qb = {key: jnp.broadcast_to(q[key][g : g + 1], (8, 128)) for key in q}
        for c in range(8):
            x = [t_ref[g * 4 + u, c * 8 : c * 8 + 8, :] for u in range(4)]
            y = [t_ref[g * 4 + u, 64 + c * 8 : 72 + c * 8, :] for u in range(4)]
            for u in range(4):
                fx = pb[u, u] * x[u]
                fy = pb[u, u] * y[u]
                for w in range(4):
                    if w != u:
                        key = (min(u, w), max(u, w))
                        fx = fx + pb[key] * x[w]
                        fy = fy + pb[key] * y[w]
                        if u < w:
                            fx = fx + qb[key] * y[w]
                            fy = fy - qb[key] * x[w]
                        else:
                            fx = fx - qb[key] * y[w]
                            fy = fy + qb[key] * x[w]
                f_ref[g * 4 + u, c * 8 : c * 8 + 8, :] = fx
                f_ref[g * 4 + u, 64 + c * 8 : 72 + c * 8, :] = fy
    for i in range(8):
        w_ref[i] = f_ref[i].T

    sub = lax.broadcasted_iota(jnp.int32, (128, 128), 0)
    lane = lax.broadcasted_iota(jnp.int32, (128, 128), 1)
    lane_u = (lane[:1] // 8) % 4
    wanted = aux_ref[2:3].astype(jnp.int32)
    row_u, row_g = sub % 4, (sub // 4) % 2
    own = lane[:16] // 8 == lax.broadcasted_iota(jnp.int32, (16, 128), 0)
    total = jnp.zeros((256, 128), F32)
    for m in range(8):
        pick = jnp.where((wanted == 2 * m + row_g) & (lane_u == row_u), 1.0, 0.0).astype(BF16)
        rows = []
        for f in range(16):
            at = m * 144 + 128 + f
            row = jnp.broadcast_to(x_ref[at : at + 1, :], (16, 128))
            rows.append(jnp.where(own, row, 0.0).astype(BF16))
        total = total + jnp.dot(jnp.concatenate(rows, axis=0), pick, preferred_element_type=F32)
    upper = jnp.floor(total * 0.25)
    re = 2.0 * (total - 4.0 * upper) - 3.0
    im = 2.0 * upper - 3.0
    for f in range(16):
        s_ref[f * 32 : f * 32 + 16, :] = re[f * 16 : f * 16 + 16]
        s_ref[f * 32 + 16 : f * 32 + 32, :] = im[f * 16 : f * 16 + 16]


def cancel_kernel(half, v_ref, w_ref, s_ref, y_ref, order_ref, out_ref, ys_ref, yf_ref, e_ref, sem):
    start = half * 8
    first = pl.multiple_of(lax.axis_index("section") * 16 + start, 8)
    copy = pltpu.make_async_copy(y_ref.at[:, pl.ds(first, 8), :], ys_ref.at[pl.ds(0, 14)], sem)
    copy.start()
    ys_ref[14:16] = jnp.zeros((2, 8, 128), F32)
    row = lax.broadcasted_iota(jnp.int32, (64, 128), 0)
    col = lax.broadcasted_iota(jnp.int32, (64, 128), 1)
    earlier = 2 * (row % 8) + row // 32 < 2 * (col % 8) + (col // 32) % 2
    sign = jnp.where(col[:1] < 64, -1.0, 1.0)
    copy.wait()
    yf_ref[...] = ys_ref[...].reshape(128, 128)
    nt = (((1,), (1,)), ((), ()))
    for f in range(8):
        at = slice((start + f) * 8, (start + f) * 8 + 8)
        filt = jnp.concatenate([w_ref[i, at, :] for i in range(8)], axis=0)
        filt = jnp.concatenate([filt, pltpu.roll(filt, 64, 1) * sign], axis=0)
        fh = filt.astype(BF16)
        fl = (filt - fh.astype(F32)).astype(BF16)
        left = jnp.concatenate([v_ref[i, at, :] for i in range(8)] + [yf_ref[pl.ds(f, 16, stride=8), :]], axis=0)
        lh = left.astype(BF16)
        ll = (left - lh.astype(F32)).astype(BF16)
        xz = lax.dot_general(lh, fh, nt, preferred_element_type=F32)
        xz = xz + lax.dot_general(lh, fl, nt, preferred_element_type=F32)
        xz = xz + lax.dot_general(ll, fh, nt, preferred_element_type=F32)
        cross = jnp.where(earlier, xz[:64], 0.0)
        ch = cross.astype(BF16)
        cl = (cross - ch.astype(F32)).astype(BF16)
        sym = s_ref[(start + f) * 32 : (start + f) * 32 + 32, :64].astype(BF16)
        gone = jnp.dot(sym, ch, preferred_element_type=F32) + jnp.dot(sym, cl, preferred_element_type=F32)
        gone = gone[:16] + pltpu.roll(gone[16:], 64, 1) * sign
        e_ref[pl.ds(f, 16, stride=8), :] = xz[64:] - gone * (1.0 / ROOT_TEN)
    turned = e_ref[...].T
    for c in range(2):
        for g in range(2):
            for u in range(4):
                at = (c * 8 + g * 4 + u) * 8
                out_ref[pl.ds(g * 8 + c * 4 + u, 8, stride=16), :] = turned[at : at + 8, :]


def pack_kernel(one_ref, two_ref, order_ref, out_ref):
    for m in range(8):
        out_ref[m, 0] = one_ref[m * 16 : m * 16 + 16, :]
        out_ref[m, 1] = two_ref[m * 16 : m * 16 + 16, :]


def finish_kernel(count, est_ref, gain_ref, out_ref):
    total = jnp.sum(gain_ref[...], axis=1, keepdims=True)
    recip = count / total
    block = lax.broadcasted_iota(jnp.int32, (8, 128), 1) // 8
    for g in range(2):
        users = [recip[u * 2 + g : u * 2 + g + 1] for u in range(4)]
        scale = jnp.broadcast_to(jnp.concatenate(users + users, axis=0), (8, 128))
        x = [est_ref[i // 2, i % 2, g * 8 : g * 8 + 8, :] for i in range(16)]
        for bit in (1, 2, 4, 8):
            low = (block & bit) == 0
            new = list(x)
            for i in range(16):
                if i & bit == 0:
                    j = i | bit
                    new[i] = jnp.where(low, x[i], pltpu.roll(x[j], 8 * bit, 1))
                    new[j] = jnp.where(low, pltpu.roll(x[i], 128 - 8 * bit, 1), x[j])
            x = new
        for t in range(14):
            out_ref[t, g * 8 : g * 8 + 8, :] = x[t] * scale


def halo(h):
    size = lax.axis_size("sc")
    even = lax.axis_index("sc") % 2 == 0
    close = [(i, i ^ 1) for i in range(size)]
    far = [(i, i + 1) for i in range(1, size - 1, 2)]
    far = far + [(j, i) for i, j in far]
    far = lax.ppermute(jnp.where(even, h[:1], h[-1:]), "sc", far)
    close = lax.ppermute(jnp.where(even, h[-1:], h[:1]), "sc", close)
    return close, far


def over_sections(x):
    return lax.all_to_all(x, "section", split_axis=0, concat_axis=0, tiled=True)


def from_partner(x, bit):
    return lax.ppermute(x, "sc", [(i, i ^ bit) for i in range(lax.axis_size("sc"))])


def kernel(body, shape, in_specs, name, scratch=(), aliases=None, flops=0, moved=0):
    out = [jax.ShapeDtypeStruct(s, F32) for s in shape] if isinstance(shape, list) else jax.ShapeDtypeStruct(shape, F32)
    return pl.pallas_call(
        body,
        out_shape=out,
        in_specs=in_specs,
        out_specs=[VMEM] * len(shape) if isinstance(shape, list) else VMEM,
        scratch_shapes=list(scratch),
        input_output_aliases=aliases or {},
        compiler_params=PARAMS,
        cost_estimate=pl.CostEstimate(flops=flops, bytes_accessed=moved, transcendentals=0),
        name=name,
    )


def local(observed_vector, propagation_matrix, noise_var, sliced_constellation, detection_sequence):
    h = propagation_matrix.reshape(128, 8, 128)
    noise = noise_var.reshape(1, 128)
    labels = sliced_constellation.transpose(1, 2, 0).reshape(112, 128)
    y = observed_vector.transpose(1, 0, 2)
    big = (8, 128, 128)
    smem = pl.BlockSpec(memory_space=pltpu.SMEM)
    close, far = halo(h)
    inner, aux = kernel(inner_kernel, [(8, 144, 128), (8, 128)], [smem] + [VMEM] * 3, "inner", flops=10**6, moved=2 * 10**6)(
        detection_sequence, h, labels, noise
    )
    smooth = kernel(edge_kernel, (8, 144, 128), [VMEM] * 3, "edge")(inner, close, far)
    gathered = over_sections(smooth)
    gain = kernel(gain_kernel, (8, 128), [VMEM] * 4, "gain", [pltpu.VMEM(big, F32)], flops=10**6, moved=10**6)(inner, close, far, aux)

    def add(name, x, other, after):
        return kernel(add_kernel, (8, 128), [VMEM, VMEM, ANY], name)(x, other, after)

    def cancel(half, *args):
        scratch = [pltpu.VMEM((16, 8, 128), F32), pltpu.VMEM((128, 128), F32), pltpu.VMEM((128, 128), F32), pltpu.SemaphoreType.DMA]
        body = lambda *refs: cancel_kernel(half, *refs)
        specs = [VMEM, VMEM, VMEM, ANY, ANY]
        return kernel(body, (128, 128), specs, "cancel", scratch, flops=10**8, moved=4 * 10**6)(*args)

    gain = gain + from_partner(gain, 16)
    gain = add("add_a", gain, from_partner(gain, 1), gathered)
    tiles, filters, symbols = kernel(
        filter_kernel,
        [big, big, (512, 128)],
        [VMEM, VMEM, ANY],
        "filters",
        [pltpu.VMEM(big, F32), pltpu.VMEM(big, F32)],
        flops=10**8,
        moved=4 * 10**6,
    )(gathered.reshape(1152, 128), aux, gain)
    one = cancel(0, tiles, filters, symbols, y, gain)
    gain = add("add_b", gain, from_partner(gain, 2), one)
    two = cancel(1, tiles, filters, symbols, y, gain)
    gain = add("add_c", gain, from_partner(gain, 8), two)
    estimates = kernel(pack_kernel, (8, 2, 16, 128), [VMEM, VMEM, ANY], "pack")(one, two, gain)
    estimates = over_sections(estimates)
    gain = gain + from_partner(gain, 4)
    count = float(128 * lax.axis_size("sc"))
    body = lambda *refs: finish_kernel(count, *refs)
    out = kernel(body, (14, 16, 128), [VMEM] * 2, "finish")(estimates, gain)
    return out.transpose(2, 0, 1)


def solution(mesh):
    in_specs = (
        P("sc", None, None),
        P("sc", "section", None, None),
        P("sc"),
        P("sc", None, "section"),
        P(),
    )
    out_specs = P("sc", None, "section")
    return jax.shard_map(local, mesh=mesh, in_specs=in_specs, out_specs=out_specs, check_vma=False)
```

time: 64.4 us -> 49.1 us (0.76)
  blocking collectives: 13.2 us -> 0 us
  waiting for transfers between devices: 11.9 us -> 9.41 us
  Pallas kernels: 6.59 us -> 8.15 us
  local copies, waits for them, and re-layouts: 3.24 us -> 1.7 us
  other arithmetic: 0.02 us -> 0.72 us
    all_to_all x1 -> x0, blocking collectives: 13.2 us -> none  [over_sections(): return lax.all_to_all(x, 'section', split_axis=0, concat_axis=0, tiled=True)]
    ppermute x7, starting transfers between devices: 24.1 us -> 17.1 us  [the longest x5 16.5 us: from_partner(): lax.ppermute(x, 'sc', [(i, i ^ bit) for i in range(lax.axis_size('sc'))])]
    all_to_all x1 -> x2, starting transfers between devices: 4.92 us -> 11.5 us  [over_sections(): return lax.all_to_all(x, 'section', split_axis=0, concat_axis=0, tiled=True)]
    ppermute x7, waiting for transfers between devices: 11.9 us -> 7.6 us  [the longest x5 7.59 us: from_partner(): lax.ppermute(x, 'sc', [(i, i ^ bit) for i in range(lax.axis_size('sc'))])]
    all_to_all x1 -> x2, waiting for transfers between devices: 0.01 us -> 1.81 us  [over_sections(): return lax.all_to_all(x, 'section', split_axis=0, concat_axis=0, tiled=True)]
    pallas_call x4 -> x11, Pallas kernels: 6.59 us -> 8.15 us  [the longest x2 3.87 us: cancel(): kernel(body, (128, 128), specs, 'cancel', scratch, flops=10 ** 8, moved=4...]
    unnamed x10, local copies, waits for them, and re-layouts: 2.53 us -> 1.7 us
    select_n x0 -> x1, other arithmetic: none -> 0.71 us  [halo(): far = lax.ppermute(jnp.where(even, h[:1], h[-1:]), 'sc', far)]
  transfers between devices with their start and end apart: 8 -> 9, of which waited for: 6 -> 6; matrix products, arithmetic and copies ran while one was open for 0% -> 0% of each run, Pallas kernels for 0% -> 12%
where the time goes in v2:
time: 49.1 us; the launch traced here: 48.7 us
  starting transfers between devices  28.7 us (58%)
  waiting for transfers between devices  9.41 us (19%)
  Pallas kernels  8.15 us (17%)
  local copies, waits for them, and re-layouts  1.7 us (3%)
  other arithmetic  0.72 us (1%)
    ppermute x5, starting transfers between devices, from_partner(): lax.ppermute(x, 'sc', [(i, i ^ bit) for i in range(lax.axis_size('sc'))])  16.5 us
    all_to_all x2, starting transfers between devices, over_sections(): return lax.all_to_all(x, 'section', split_axis=0, concat_axis=0, tiled=True)  11.5 us
    ppermute x5, waiting for transfers between devices, from_partner(): lax.ppermute(x, 'sc', [(i, i ^ bit) for i in range(lax.axis_size('sc'))])  7.59 us
    pallas_call x2, Pallas kernels, cancel(): kernel(body, (128, 128), specs, 'cancel', scratch, flops=10 ** 8, moved=4...  3.87 us
    all_to_all x2, waiting for transfers between devices, over_sections(): return lax.all_to_all(x, 'section', split_axis=0, concat_axis=0, tiled=True)  1.81 us
    unnamed x10, local copies, waits for them, and re-layouts  1.7 us
  transfers between devices with their start and end apart: 9, of which 6 were waited for; matrix products, arithmetic and copies ran while one was open for 0% of the time, Pallas kernels for 12%

profile of v2, /device:TPU:2, one launch (start us, length us, event | category | flops | bytes accessed | tf_op | source)
XLA Modules:
  0.0 48.7 jit_solution(7316040099328623846)
XLA Ops:
  0.0 0.0 copy-start.2
  0.0 0.7 %slice_select_fusion = (f32[1,2,4,128]{3,2,1,0:T(4,128)S(1)}, f32[1,2,4,128]{3,2,1,0:T(4,128)S(1)}) fusion(f32[128,2,4,128]{3,2,1,0:T(4,128)} %param.6, pred[]{:T(512)S(6)} %eq.5), kind=kLoop, calls=%fused_computation | loop fusion | flops 2048 | bytes 16385 | tf_op jit(solution)/shard_map/jit(_where)/select_n | solution.py:273
  0.7 0.0 collective-permute-start
  0.7 0.7 %collective-permute-start.1 = (f32[1,8,128]{2,1,0:T(8,128)S(1)}, f32[1,8,128]{2,1,0:T(8,128)S(1)}, u32[]{:S(2)}, u32[]{:S(2)}) collective-permute-start(f32[1,8,128]{2,1,0:T(8,128)S(1)} %bitcast.16), channel_id=1, source_target_pairs={{1,2},{3,4},{5,6},{7,8},{9,10},{11,12},{13,14},{15,16},{17,18},{19... | collective-permute-start | bytes 12296 | tf_op jit(solution)/shard_map/ppermute | solution.py:273
  1.4 0.0 copy-start.3
  1.4 0.0 copy-start.4
  1.4 0.0 copy-done.2
  1.4 0.6 %copy-done.3 = s32[16]{0:T(128)S(1)} copy-done((s32[16]{0:T(128)S(1)}, s32[16]{0:T(128)}, u32[]{:S(2)}) %copy-start.3) | copy-done | bytes 88
  2.0 0.0 copy-done.4
  2.1 0.0 copy-start.1
  2.1 1.0 %copy-done.1 = f32[128,2,4,128]{3,2,1,0:T(4,128)S(1)} copy-done((f32[128,2,4,128]{3,2,1,0:T(4,128)S(1)}, f32[128,2,4,128]{3,2,1,0:T(4,128)}, u32[]{:S(2)}) %copy-start.1) | copy-done | bytes 524312
  3.1 0.6 %inner.1 = (f32[8,144,128]{2,1,0:T(8,128)S(1)}, f32[8,128]{1,0:T(8,128)S(1)}) custom-call(s32[16]{0:T(128)S(1)} %copy-done.3, f32[128,8,128]{2,1,0:T(8,128)S(1)} %bitcast.13, s32[112,128]{1,0:T(8,128)S(1)} %bitcast.14, f32[1,128]{1,0:T(1,128)S(1)} %bitcast.15), custom_call_target="tpu_custom_call" | custom-call | flops 1000000 | bytes 2000000 | tf_op jit(solution)/shard_map/inner/pallas_call | solution.py:309
  3.7 0.0 collective-permute-done.close_ref
  3.8 0.0 collective-permute-done.1.far_ref
  3.8 0.9 %edge.1 = f32[8,144,128]{2,1,0:T(8,128)} custom-call(f32[8,144,128]{2,1,0:T(8,128)S(1)} %get-tuple-element.10.x_ref, f32[1,8,128]{2,1,0:T(8,128)S(1)} %collective-permute-done.close_ref, f32[1,8,128]{2,1,0:T(8,128)S(1)} %collective-permute-done.1.far_ref), custom_call_target="tpu_custom_call" | custom-call | tf_op jit(solution)/shard_map/edge/pallas_call | solution.py:312
  4.6 5.8 %all-to-all-start = ((f32[8,144,128]{2,1,0:T(8,128)}), f32[8,144,128]{2,1,0:T(8,128)S(1)}, u32[]{:S(2)}, u32[]{:S(2)}) async-start(f32[8,144,128]{2,1,0:T(8,128)} %edge.1), calls=%async_computation | async-start | bytes 1179648 | tf_op jit(solution)/shard_map/all_to_all | solution.py:279
  10.5 0.0 copy-start
  10.5 0.3 gain.1
  10.8 12.8 %collective-permute-start.2 = (f32[8,128]{1,0:T(8,128)S(1)}, f32[8,128]{1,0:T(8,128)S(1)}, u32[]{:S(2)}, u32[]{:S(2)}) collective-permute-start(f32[8,128]{1,0:T(8,128)S(1)} %gain.1), channel_id=1, source_target_pairs={{0,16},{1,17},{2,18},{3,19},{4,20},{5,21},{6,22},{7,23},{8,24},{9,... | collective-permute-start | bytes 12296 | tf_op jit(solution)/shard_map/ppermute | solution.py:283
  23.6 1.6 %collective-permute-done.2 = f32[8,128]{1,0:T(8,128)S(1)} collective-permute-done((f32[8,128]{1,0:T(8,128)S(1)}, f32[8,128]{1,0:T(8,128)S(1)}, u32[]{:S(2)}, u32[]{:S(2)}) %collective-permute-start.2) | collective-permute-done | bytes 4128 | tf_op jit(solution)/shard_map/ppermute | solution.py:283
  25.2 0.0 collective-permute-start.3
  25.2 1.2 %collective-permute-done.3.other_ref = f32[8,128]{1,0:T(8,128)S(1)} collective-permute-done((f32[8,128]{1,0:T(8,128)S(1)}, f32[8,128]{1,0:T(8,128)S(1)}, u32[]{:S(2)}, u32[]{:S(2)}) %collective-permute-start.3) | collective-permute-done | bytes 4128 | tf_op jit(solution)/shard_map/ppermute | solution.py:283
  26.3 0.0 all-to-all-done.order_ref
  26.3 1.3 %collective-permute-start.4 = (f32[8,128]{1,0:T(8,128)S(1)}, f32[8,128]{1,0:T(8,128)S(1)}, u32[]{:S(2)}, u32[]{:S(2)}) collective-permute-start(f32[8,128]{1,0:T(8,128)S(1)} %add_a.1.order_ref.refs_4_.x_ref), channel_id=1, source_target_pairs={{0,2},{1,3},{2,0},{3,1},{4,6},{5,7},{6,4},{7,5},{8,10},{9,11},{10,... | collective-permute-start | bytes 12296 | tf_op jit(solution)/shard_map/ppermute | solution.py:283
  27.6 0.8 %filters.1 = (f32[8,128,128]{2,1,0:T(8,128)S(1)}, f32[8,128,128]{2,1,0:T(8,128)S(1)}, f32[512,128]{1,0:T(8,128)S(1)}) custom-call(f32[1152,128]{1,0:T(8,128)S(1)} %bitcast.10, f32[8,128]{1,0:T(8,128)S(1)} %get-tuple-element.11.aux_ref, f32[8,128]{1,0:T(8,128)S(1)} %add_a.1.order_ref.refs_4_.x_ref), custom_call_target="tpu_custom_call" | custom-call | flops 100000000 | bytes 4000000 | tf_op jit(solution)/shard_map/filters/pallas_call | solution.py:327
  28.4 0.0 copy-done
  28.4 1.9 %cancel.2.order_ref.one_ref = f32[128,128]{1,0:T(8,128)S(1)} custom-call(f32[8,128,128]{2,1,0:T(8,128)S(1)} %get-tuple-element.12.refs_0_, f32[8,128,128]{2,1,0:T(8,128)S(1)} %get-tuple-element.13.refs_1_, f32[512,128]{1,0:T(8,128)S(1)} %get-tuple-element.14.refs_2_, f32[14,128,128]{2,1,0:T(8,128)S(1)} %bitcast.11, f32[8,128]{1,0:T(8,128)S(1)} %add_a.1.order_ref.refs_4_.x_ref), custom_call_target="tpu_custom_call" | custom-call | flops 100000000 | bytes 4000000 | tf_op jit(solution)/shard_map/cancel/pallas_call | solution.py:323
  30.3 1.1 %collective-permute-done.4.other_ref = f32[8,128]{1,0:T(8,128)S(1)} collective-permute-done((f32[8,128]{1,0:T(8,128)S(1)}, f32[8,128]{1,0:T(8,128)S(1)}, u32[]{:S(2)}, u32[]{:S(2)}) %collective-permute-start.4) | collective-permute-done | bytes 4128 | tf_op jit(solution)/shard_map/ppermute | solution.py:283
  31.5 2.3 %collective-permute-start.5 = (f32[8,128]{1,0:T(8,128)S(1)}, f32[8,128]{1,0:T(8,128)S(1)}, u32[]{:S(2)}, u32[]{:S(2)}) collective-permute-start(f32[8,128]{1,0:T(8,128)S(1)} %add_b.1.refs_4_.x_ref), channel_id=1, source_target_pairs={{0,8},{1,9},{2,10},{3,11},{4,12},{5,13},{6,14},{7,15},{8,0},{9,1},... | collective-permute-start | bytes 12296 | tf_op jit(solution)/shard_map/ppermute | solution.py:283
  33.7 1.9 %cancel.3.order_ref.two_ref = f32[128,128]{1,0:T(8,128)S(1)} custom-call(f32[8,128,128]{2,1,0:T(8,128)S(1)} %get-tuple-element.12.refs_0_, f32[8,128,128]{2,1,0:T(8,128)S(1)} %get-tuple-element.13.refs_1_, f32[512,128]{1,0:T(8,128)S(1)} %get-tuple-element.14.refs_2_, f32[14,128,128]{2,1,0:T(8,128)S(1)} %bitcast.12, f32[8,128]{1,0:T(8,128)S(1)} %add_b.1.refs_4_.x_ref), custom_call_target="tpu_custom_call" | custom-call | flops 100000000 | bytes 4000000 | tf_op jit(solution)/shard_map/cancel/pallas_call | solution.py:323
  35.7 0.3 collective-permute-done.5.other_ref
  36.0 0.7 %pack.1 = f32[8,2,16,128]{3,2,1,0:T(8,128)} custom-call(f32[128,128]{1,0:T(8,128)S(1)} %cancel.2.order_ref.one_ref, f32[128,128]{1,0:T(8,128)S(1)} %cancel.3.order_ref.two_ref, f32[8,128]{1,0:T(8,128)S(1)} %add_c.1.order_ref), custom_call_target="tpu_custom_call" | custom-call | tf_op jit(solution)/shard_map/pack/pallas_call | solution.py:340
  36.6 5.7 %all-to-all-start.1 = ((f32[8,2,16,128]{3,2,1,0:T(8,128)}), f32[8,2,16,128]{3,2,1,0:T(8,128)S(1)}, u32[]{:S(2)}, u32[]{:S(2)}) async-start(f32[8,2,16,128]{3,2,1,0:T(8,128)} %pack.1), calls=%async_computation.1 | async-start | bytes 262144 | tf_op jit(solution)/shard_map/all_to_all | solution.py:279
  42.4 0.2 collective-permute-start.6
  42.5 3.4 %collective-permute-done.6 = f32[8,128]{1,0:T(8,128)S(1)} collective-permute-done((f32[8,128]{1,0:T(8,128)S(1)}, f32[8,128]{1,0:T(8,128)S(1)}, u32[]{:S(2)}, u32[]{:S(2)}) %collective-permute-start.6) | collective-permute-done | bytes 4128 | tf_op jit(solution)/shard_map/ppermute | solution.py:283
  46.0 1.8 %all-to-all-done.1.refs_0_ = f32[8,2,16,128]{3,2,1,0:T(8,128)S(1)} async-done(((f32[8,2,16,128]{3,2,1,0:T(8,128)}), f32[8,2,16,128]{3,2,1,0:T(8,128)S(1)}, u32[]{:S(2)}, u32[]{:S(2)}) %all-to-all-start.1) | async-done | bytes 131104 | tf_op jit(solution)/shard_map/all_to_all | solution.py:279
  47.8 1.0 %finish.1 = f32[14,16,128]{2,1,0:T(8,128)} custom-call(f32[8,2,16,128]{3,2,1,0:T(8,128)S(1)} %all-to-all-done.1.refs_0_, f32[8,128]{1,0:T(8,128)S(1)} %add.12.refs_1_), custom_call_target="tpu_custom_call" | custom-call | tf_op jit(solution)/shard_map/finish/pallas_call | solution.py:345
  (5 shorter events, 0.0 us)
Async XLA Ops:
  0.0 1.4 %copy-start.2 = (s32[128,14,8]{0,2,1:T(8,128)S(1)}, s32[128,14,8]{0,2,1:T(8,128)}, u32[]{:S(2)}) copy-start(s32[128,14,8]{0,2,1:T(8,128)} %param.8) | copy-start | bytes 172036
  0.7 3.0 %collective-permute-start = (f32[1,8,128]{2,1,0:T(8,128)S(1)}, f32[1,8,128]{2,1,0:T(8,128)S(1)}, u32[]{:S(2)}, u32[]{:S(2)}) collective-permute-start(f32[1,8,128]{2,1,0:T(8,128)S(1)} %bitcast.17), channel_id=1, source_target_pairs={{0,1},{1,0},{2,3},{3,2},{4,5},{5,4},{6,7},{7,6},{8,9},{9,8},{10,11... | collective-permute-start | bytes 12296 | tf_op jit(solution)/shard_map/ppermute | solution.py:274
  0.7 3.0 %collective-permute-start.1 = (f32[1,8,128]{2,1,0:T(8,128)S(1)}, f32[1,8,128]{2,1,0:T(8,128)S(1)}, u32[]{:S(2)}, u32[]{:S(2)}) collective-permute-start(f32[1,8,128]{2,1,0:T(8,128)S(1)} %bitcast.16), channel_id=1, source_target_pairs={{1,2},{3,4},{5,6},{7,8},{9,10},{11,12},{13,14},{15,16},{17,18},{19... | collective-permute-start | bytes 12296 | tf_op jit(solution)/shard_map/ppermute | solution.py:273
  1.4 0.7 %copy-start.3 = (s32[16]{0:T(128)S(1)}, s32[16]{0:T(128)}, u32[]{:S(2)}) copy-start(s32[16]{0:T(128)} %seq_ref.1) | copy-start | bytes 196
  1.4 0.7 %copy-start.4 = (f32[128]{0:T(128)S(1)}, f32[128]{0:T(128)}, u32[]{:S(2)}) copy-start(f32[128]{0:T(128)} %param.7) | copy-start | bytes 1540
  2.1 1.0 %copy-start.1 = (f32[128,2,4,128]{3,2,1,0:T(4,128)S(1)}, f32[128,2,4,128]{3,2,1,0:T(4,128)}, u32[]{:S(2)}) copy-start(f32[128,2,4,128]{3,2,1,0:T(4,128)} %param.6) | copy-start | bytes 1572868
  4.6 21.7 %all-to-all-start = ((f32[8,144,128]{2,1,0:T(8,128)}), f32[8,144,128]{2,1,0:T(8,128)S(1)}, u32[]{:S(2)}, u32[]{:S(2)}) async-start(f32[8,144,128]{2,1,0:T(8,128)} %edge.1), calls=%async_computation | async-start | bytes 1179648 | tf_op jit(solution)/shard_map/all_to_all | solution.py:279
  10.5 17.9 %copy-start = (f32[128,14,128]{2,0,1:T(8,128)S(1)}, f32[128,14,128]{2,0,1:T(8,128)}, u32[]{:S(2)}) copy-start(f32[128,14,128]{2,0,1:T(8,128)} %param.5) | copy-start | bytes 2752516
  10.8 14.3 %collective-permute-start.2 = (f32[8,128]{1,0:T(8,128)S(1)}, f32[8,128]{1,0:T(8,128)S(1)}, u32[]{:S(2)}, u32[]{:S(2)}) collective-permute-start(f32[8,128]{1,0:T(8,128)S(1)} %gain.1), channel_id=1, source_target_pairs={{0,16},{1,17},{2,18},{3,19},{4,20},{5,21},{6,22},{7,23},{8,24},{9,... | collective-permute-start | bytes 12296 | tf_op jit(solution)/shard_map/ppermute | solution.py:283
  25.2 1.2 %collective-permute-start.3 = (f32[8,128]{1,0:T(8,128)S(1)}, f32[8,128]{1,0:T(8,128)S(1)}, u32[]{:S(2)}, u32[]{:S(2)}) collective-permute-start(f32[8,128]{1,0:T(8,128)S(1)} %add.11.x_ref), channel_id=1, source_target_pairs={{0,1},{1,0},{2,3},{3,2},{4,5},{5,4},{6,7},{7,6},{8,9},{9,8},{10,11... | collective-permute-start | bytes 12296 | tf_op jit(solution)/shard_map/ppermute | solution.py:283
  26.3 5.1 %collective-permute-start.4 = (f32[8,128]{1,0:T(8,128)S(1)}, f32[8,128]{1,0:T(8,128)S(1)}, u32[]{:S(2)}, u32[]{:S(2)}) collective-permute-start(f32[8,128]{1,0:T(8,128)S(1)} %add_a.1.order_ref.refs_4_.x_ref), channel_id=1, source_target_pairs={{0,2},{1,3},{2,0},{3,1},{4,6},{5,7},{6,4},{7,5},{8,10},{9,11},{10,... | collective-permute-start | bytes 12296 | tf_op jit(solution)/shard_map/ppermute | solution.py:283
  31.5 4.5 %collective-permute-start.5 = (f32[8,128]{1,0:T(8,128)S(1)}, f32[8,128]{1,0:T(8,128)S(1)}, u32[]{:S(2)}, u32[]{:S(2)}) collective-permute-start(f32[8,128]{1,0:T(8,128)S(1)} %add_b.1.refs_4_.x_ref), channel_id=1, source_target_pairs={{0,8},{1,9},{2,10},{3,11},{4,12},{5,13},{6,14},{7,15},{8,0},{9,1},... | collective-permute-start | bytes 12296 | tf_op jit(solution)/shard_map/ppermute | solution.py:283
  36.6 11.1 %all-to-all-start.1 = ((f32[8,2,16,128]{3,2,1,0:T(8,128)}), f32[8,2,16,128]{3,2,1,0:T(8,128)S(1)}, u32[]{:S(2)}, u32[]{:S(2)}) async-start(f32[8,2,16,128]{3,2,1,0:T(8,128)} %pack.1), calls=%async_computation.1 | async-start | bytes 262144 | tf_op jit(solution)/shard_map/all_to_all | solution.py:279
  42.4 3.6 %collective-permute-start.6 = (f32[8,128]{1,0:T(8,128)S(1)}, f32[8,128]{1,0:T(8,128)S(1)}, u32[]{:S(2)}, u32[]{:S(2)}) collective-permute-start(f32[8,128]{1,0:T(8,128)S(1)} %add_c.1.order_ref), channel_id=1, source_target_pairs={{0,4},{1,5},{2,6},{3,7},{4,0},{5,1},{6,2},{7,3},{8,12},{9,13},{10,... | collective-permute-start | bytes 12296 | tf_op jit(solution)/shard_map/ppermute | solution.py:283

commit v3 on v2

--- a/solution.py
+++ b/solution.py
@@ -10,6 +10,7 @@
 BF16 = jnp.bfloat16
 VMEM = pl.BlockSpec(memory_space=pltpu.VMEM)
 ANY = pl.BlockSpec(memory_space=pl.ANY)
+SMEM = pl.BlockSpec(memory_space=pltpu.SMEM)
 PARAMS = pltpu.CompilerParams(vmem_limit_bytes=32 * 1024 * 1024)
 
 
@@ -123,6 +124,11 @@
     out_ref[...] = x_ref[...] + other_ref[...]
 
 
+def pack_kernel(x_ref, gain_ref, other_ref, out_ref, sum_ref):
+    out_ref[...] = x_ref[...]
+    sum_ref[...] = gain_ref[...] + other_ref[...]
+
+
 def gain_kernel(x_ref, close_ref, far_ref, aux_ref, out_ref, t_ref):
     even = lax.axis_index("sc") % 2 == 0
     close, far = close_ref[0], far_ref[0]
@@ -197,71 +203,72 @@
         s_ref[f * 32 + 16 : f * 32 + 32, :] = im[f * 16 : f * 16 + 16]
 
 
-def cancel_kernel(half, v_ref, w_ref, s_ref, y_ref, order_ref, out_ref, ys_ref, yf_ref, e_ref, sem):
-    start = half * 8
-    first = pl.multiple_of(lax.axis_index("section") * 16 + start, 8)
-    copy = pltpu.make_async_copy(y_ref.at[:, pl.ds(first, 8), :], ys_ref.at[pl.ds(0, 14)], sem)
+def cancel_kernel(v_ref, w_ref, s_ref, y_ref, out_ref, ys_ref, yf_ref, e_ref, xz_ref, sem):
+    first = pl.multiple_of(lax.axis_index("section") * 16, 16)
+    copy = pltpu.make_async_copy(y_ref.at[:, pl.ds(first, 16), :], ys_ref.at[pl.ds(0, 14)], sem)
     copy.start()
-    ys_ref[14:16] = jnp.zeros((2, 8, 128), F32)
+    ys_ref[14:16] = jnp.zeros((2, 16, 128), F32)
     row = lax.broadcasted_iota(jnp.int32, (64, 128), 0)
     col = lax.broadcasted_iota(jnp.int32, (64, 128), 1)
     earlier = 2 * (row % 8) + row // 32 < 2 * (col % 8) + (col // 32) % 2
     sign = jnp.where(col[:1] < 64, -1.0, 1.0)
     copy.wait()
-    yf_ref[...] = ys_ref[...].reshape(128, 128)
+    yf_ref[...] = ys_ref[...].reshape(256, 128)
     nt = (((1,), (1,)), ((), ()))
-    for f in range(8):
-        at = slice((start + f) * 8, (start + f) * 8 + 8)
+    for f in range(16):
+        at = slice(f * 8, f * 8 + 8)
         filt = jnp.concatenate([w_ref[i, at, :] for i in range(8)], axis=0)
         filt = jnp.concatenate([filt, pltpu.roll(filt, 64, 1) * sign], axis=0)
         fh = filt.astype(BF16)
         fl = (filt - fh.astype(F32)).astype(BF16)
-        left = jnp.concatenate([v_ref[i, at, :] for i in range(8)] + [yf_ref[pl.ds(f, 16, stride=8), :]], axis=0)
+        left = jnp.concatenate([v_ref[i, at, :] for i in range(8)] + [yf_ref[pl.ds(f, 16, stride=16), :]], axis=0)
         lh = left.astype(BF16)
         ll = (left - lh.astype(F32)).astype(BF16)
-        xz = lax.dot_general(lh, fh, nt, preferred_element_type=F32)
-        xz = xz + lax.dot_general(lh, fl, nt, preferred_element_type=F32)
+        xz = lax.dot_general(
+            jnp.concatenate([lh, lh], axis=1), jnp.concatenate([fh, fl], axis=1), nt, preferred_element_type=F32
+        )
         xz = xz + lax.dot_general(ll, fh, nt, preferred_element_type=F32)
-        cross = jnp.where(earlier, xz[:64], 0.0)
+        xz_ref[f, 0:64] = jnp.where(earlier, xz[:64], 0.0)
+        xz_ref[f, 64:80] = xz[64:]
+    for f in range(16):
+        cross = xz_ref[f, 0:64]
         ch = cross.astype(BF16)
         cl = (cross - ch.astype(F32)).astype(BF16)
-        sym = s_ref[(start + f) * 32 : (start + f) * 32 + 32, :64].astype(BF16)
-        gone = jnp.dot(sym, ch, preferred_element_type=F32) + jnp.dot(sym, cl, preferred_element_type=F32)
+        sym = s_ref[f * 32 : f * 32 + 32, :].astype(BF16)
+        gone = jnp.dot(sym, jnp.concatenate([ch, cl], axis=0), preferred_element_type=F32)
         gone = gone[:16] + pltpu.roll(gone[16:], 64, 1) * sign
-        e_ref[pl.ds(f, 16, stride=8), :] = xz[64:] - gone * (1.0 / ROOT_TEN)
-    turned = e_ref[...].T
-    for c in range(2):
-        for g in range(2):
-            for u in range(4):
-                at = (c * 8 + g * 4 + u) * 8
-                out_ref[pl.ds(g * 8 + c * 4 + u, 8, stride=16), :] = turned[at : at + 8, :]
-
-
-def pack_kernel(one_ref, two_ref, order_ref, out_ref):
-    for m in range(8):
-        out_ref[m, 0] = one_ref[m * 16 : m * 16 + 16, :]
-        out_ref[m, 1] = two_ref[m * 16 : m * 16 + 16, :]
+        e_ref[pl.ds(f, 16, stride=16), :] = xz_ref[f, 64:80] - gone * (1.0 / ROOT_TEN)
+    for half in range(2):
+        turned = e_ref[half * 128 : half * 128 + 128, :].T
+        for c in range(2):
+            for g in range(2):
+                for u in range(4):
+                    at = (c * 8 + g * 4 + u) * 8
+                    out_ref[pl.ds(half * 16 + g * 8 + c * 4 + u, 8, stride=32), :] = turned[at : at + 8, :]
 
 
 def finish_kernel(count, est_ref, gain_ref, out_ref):
     total = jnp.sum(gain_ref[...], axis=1, keepdims=True)
     recip = count / total
-    block = lax.broadcasted_iota(jnp.int32, (8, 128), 1) // 8
+    block = lax.broadcasted_iota(jnp.int32, (8, 128), 1) // 16
     for g in range(2):
         users = [recip[u * 2 + g : u * 2 + g + 1] for u in range(4)]
         scale = jnp.broadcast_to(jnp.concatenate(users + users, axis=0), (8, 128))
-        x = [est_ref[i // 2, i % 2, g * 8 : g * 8 + 8, :] for i in range(16)]
-        for bit in (1, 2, 4, 8):
-            low = (block & bit) == 0
-            new = list(x)
-            for i in range(16):
-                if i & bit == 0:
-                    j = i | bit
-                    new[i] = jnp.where(low, x[i], pltpu.roll(x[j], 8 * bit, 1))
-                    new[j] = jnp.where(low, pltpu.roll(x[i], 128 - 8 * bit, 1), x[j])
-            x = new
-        for t in range(14):
-            out_ref[t, g * 8 : g * 8 + 8, :] = x[t] * scale
+        for half in range(2):
+            x = [est_ref[m, half, g * 8 : g * 8 + 8, :] for m in range(8)]
+            for bit in (1, 2, 4):
+                low = (block & bit) == 0
+                new = list(x)
+                for i in range(8):
+                    if i & bit == 0:
+                        j = i | bit
+                        new[i] = jnp.where(low, x[i], pltpu.roll(x[j], 16 * bit, 1))
+                        new[j] = jnp.where(low, pltpu.roll(x[i], 128 - 16 * bit, 1), x[j])
+                x = new
+            for i in range(8):
+                t = half * 8 + i
+                if t < 14:
+                    out_ref[t, g * 8 : g * 8 + 8, :] = x[i] * scale
 
 
 def halo(h):
@@ -283,19 +290,19 @@
     return lax.ppermute(x, "sc", [(i, i ^ bit) for i in range(lax.axis_size("sc"))])
 
 
-def kernel(body, shape, in_specs, name, scratch=(), aliases=None, flops=0, moved=0):
-    out = [jax.ShapeDtypeStruct(s, F32) for s in shape] if isinstance(shape, list) else jax.ShapeDtypeStruct(shape, F32)
-    return pl.pallas_call(
+def kernel(body, shapes, in_specs, name, scratch=(), out_specs=None, aliases=None, flops=0, moved=0):
+    out = pl.pallas_call(
         body,
-        out_shape=out,
+        out_shape=[jax.ShapeDtypeStruct(shape, F32) for shape in shapes],
         in_specs=in_specs,
-        out_specs=[VMEM] * len(shape) if isinstance(shape, list) else VMEM,
+        out_specs=out_specs or [VMEM] * len(shapes),
         scratch_shapes=list(scratch),
         input_output_aliases=aliases or {},
         compiler_params=PARAMS,
         cost_estimate=pl.CostEstimate(flops=flops, bytes_accessed=moved, transcendentals=0),
         name=name,
     )
+    return lambda *args: out(*args) if len(shapes) > 1 else out(*args)[0]
 
 
 def local(observed_vector, propagation_matrix, noise_var, sliced_constellation, detection_sequence):
@@ -304,45 +311,33 @@
     labels = sliced_constellation.transpose(1, 2, 0).reshape(112, 128)
     y = observed_vector.transpose(1, 0, 2)
     big = (8, 128, 128)
-    smem = pl.BlockSpec(memory_space=pltpu.SMEM)
     close, far = halo(h)
-    inner, aux = kernel(inner_kernel, [(8, 144, 128), (8, 128)], [smem] + [VMEM] * 3, "inner", flops=10**6, moved=2 * 10**6)(
+    rows = (8, 144, 128)
+    tile = (8, 128)
+    near, aux = kernel(inner_kernel, [rows, tile], [SMEM] + [VMEM] * 3, "inner", flops=10**6, moved=2 * 10**6)(
         detection_sequence, h, labels, noise
     )
-    smooth = kernel(edge_kernel, (8, 144, 128), [VMEM] * 3, "edge")(inner, close, far)
-    gathered = over_sections(smooth)
-    gain = kernel(gain_kernel, (8, 128), [VMEM] * 4, "gain", [pltpu.VMEM(big, F32)], flops=10**6, moved=10**6)(inner, close, far, aux)
-
-    def add(name, x, other, after):
-        return kernel(add_kernel, (8, 128), [VMEM, VMEM, ANY], name)(x, other, after)
-
-    def cancel(half, *args):
-        scratch = [pltpu.VMEM((16, 8, 128), F32), pltpu.VMEM((128, 128), F32), pltpu.VMEM((128, 128), F32), pltpu.SemaphoreType.DMA]
-        body = lambda *refs: cancel_kernel(half, *refs)
-        specs = [VMEM, VMEM, VMEM, ANY, ANY]
-        return kernel(body, (128, 128), specs, "cancel", scratch, flops=10**8, moved=4 * 10**6)(*args)
-
+    gathered = over_sections(kernel(edge_kernel, [rows], [VMEM] * 3, "edge")(near, close, far))
+    scratch = [pltpu.VMEM(big, F32)]
+    gain = kernel(gain_kernel, [tile], [VMEM] * 4, "gain", scratch, flops=10**6, moved=10**6)(near, close, far, aux)
     gain = gain + from_partner(gain, 16)
-    gain = add("add_a", gain, from_partner(gain, 1), gathered)
+    gain = kernel(add_kernel, [tile], [VMEM, VMEM, ANY], "add")(gain, from_partner(gain, 1), gathered)
+    scratch = [pltpu.VMEM(big, F32), pltpu.VMEM(big, F32)]
     tiles, filters, symbols = kernel(
-        filter_kernel,
-        [big, big, (512, 128)],
-        [VMEM, VMEM, ANY],
-        "filters",
-        [pltpu.VMEM(big, F32), pltpu.VMEM(big, F32)],
-        flops=10**8,
-        moved=4 * 10**6,
+        filter_kernel, [big, big, (512, 128)], [VMEM, VMEM, ANY], "filters", scratch, flops=10**8, moved=4 * 10**6
     )(gathered.reshape(1152, 128), aux, gain)
-    one = cancel(0, tiles, filters, symbols, y, gain)
-    gain = add("add_b", gain, from_partner(gain, 2), one)
-    two = cancel(1, tiles, filters, symbols, y, gain)
-    gain = add("add_c", gain, from_partner(gain, 8), two)
-    estimates = kernel(pack_kernel, (8, 2, 16, 128), [VMEM, VMEM, ANY], "pack")(one, two, gain)
-    estimates = over_sections(estimates)
-    gain = gain + from_partner(gain, 4)
+    scratch = [pltpu.VMEM((16, 16, 128), F32), pltpu.VMEM((256, 128), F32), pltpu.VMEM((256, 128), F32)]
+    scratch += [pltpu.VMEM((16, 80, 128), F32), pltpu.SemaphoreType.DMA]
+    estimates = kernel(cancel_kernel, [(256, 128)], [VMEM, VMEM, VMEM, ANY], "cancel", scratch, flops=10**8, moved=4 * 10**6)(
+        tiles, filters, symbols, y
+    )
+    estimates, gain = kernel(pack_kernel, [(256, 128), tile], [VMEM] * 3, "pack")(estimates, gain, from_partner(gain, 2))
+    estimates = over_sections(estimates.reshape(8, 2, 16, 128))
+    gain = kernel(add_kernel, [tile], [VMEM, VMEM, ANY], "add", flops=10**10, moved=10**8)(gain, from_partner(gain, 4), aux)
+    gain = gain + from_partner(gain, 8)
     count = float(128 * lax.axis_size("sc"))
     body = lambda *refs: finish_kernel(count, *refs)
-    out = kernel(body, (14, 16, 128), [VMEM] * 2, "finish")(estimates, gain)
+    out = kernel(body, [(14, 16, 128)], [VMEM] * 2, "finish")(estimates, gain)
     return out.transpose(2, 0, 1)
 
 

time: 49.1 us -> 45.2 us (0.921)
  the two profiles are of different devices: /device:TPU:2 before, /device:TPU:32 now
where the time goes in v3:
time: 45.2 us; the launch traced here: 44.9 us
  starting transfers between devices  26.9 us (60%)
  waiting for transfers between devices  9.99 us (22%)
  Pallas kernels  5.49 us (12%)
  local copies, waits for them, and re-layouts  1.7 us (4%)
  other arithmetic  0.72 us (2%)
    ppermute x5, starting transfers between devices, from_partner(): lax.ppermute(x, 'sc', [(i, i ^ bit) for i in range(lax.axis_size('sc'))])  11.1 us
    all_to_all x2, starting transfers between devices, over_sections(): return lax.all_to_all(x, 'section', split_axis=0, concat_axis=0, tiled=True)  11 us
    ppermute x5, waiting for transfers between devices, from_partner(): lax.ppermute(x, 'sc', [(i, i ^ bit) for i in range(lax.axis_size('sc'))])  6.46 us
    pallas_call x9, Pallas kernels, kernel(): return lambda *args: out(*args) if len(shapes) > 1 else out(*args)[0]  5.49 us
    ppermute x1, starting transfers between devices, halo(): far = lax.ppermute(jnp.where(even, h[:1], h[-1:]), 'sc', far)  4.75 us
    all_to_all x2, waiting for transfers between devices, over_sections(): return lax.all_to_all(x, 'section', split_axis=0, concat_axis=0, tiled=True)  3.34 us
    unnamed x10, local copies, waits for them, and re-layouts  1.7 us
  transfers between devices with their start and end apart: 9, of which 6 were waited for; matrix products, arithmetic and copies ran while one was open for 0% of the time, Pallas kernels for 7%

profile of v3, /device:TPU:32, one launch (start us, length us, event | category | flops | bytes accessed | tf_op | source)
XLA Modules:
  0.0 44.9 jit_solution(18034948946063917422)
XLA Ops:
  0.0 0.0 copy-start.2
  0.0 0.7 %slice_select_fusion = (f32[1,2,4,128]{3,2,1,0:T(4,128)S(1)}, f32[1,2,4,128]{3,2,1,0:T(4,128)S(1)}) fusion(f32[128,2,4,128]{3,2,1,0:T(4,128)} %param.6, pred[]{:T(512)S(6)} %eq.5), kind=kLoop, calls=%fused_computation | loop fusion | flops 2048 | bytes 16385 | tf_op jit(solution)/shard_map/jit(_where)/select_n | solution.py:280
  0.7 0.0 collective-permute-start
  0.7 4.7 %collective-permute-start.1 = (f32[1,8,128]{2,1,0:T(8,128)S(1)}, f32[1,8,128]{2,1,0:T(8,128)S(1)}, u32[]{:S(2)}, u32[]{:S(2)}) collective-permute-start(f32[1,8,128]{2,1,0:T(8,128)S(1)} %bitcast.16), channel_id=1, source_target_pairs={{1,2},{3,4},{5,6},{7,8},{9,10},{11,12},{13,14},{15,16},{17,18},{19... | collective-permute-start | bytes 12296 | tf_op jit(solution)/shard_map/ppermute | solution.py:280
  5.5 0.0 copy-start.3
  5.5 0.0 copy-start.4
  5.5 0.0 copy-done.2
  5.5 0.6 %copy-done.3 = s32[16]{0:T(128)S(1)} copy-done((s32[16]{0:T(128)S(1)}, s32[16]{0:T(128)}, u32[]{:S(2)}) %copy-start.3) | copy-done | bytes 88
  6.1 0.0 copy-done.4
  6.1 0.0 copy-start.1
  6.2 1.0 %copy-done.1 = f32[128,2,4,128]{3,2,1,0:T(4,128)S(1)} copy-done((f32[128,2,4,128]{3,2,1,0:T(4,128)S(1)}, f32[128,2,4,128]{3,2,1,0:T(4,128)}, u32[]{:S(2)}) %copy-start.1) | copy-done | bytes 524312
  7.2 0.6 %inner.1 = (f32[8,144,128]{2,1,0:T(8,128)S(1)}, f32[8,128]{1,0:T(8,128)S(1)}) custom-call(s32[16]{0:T(128)S(1)} %copy-done.3, f32[128,8,128]{2,1,0:T(8,128)S(1)} %bitcast.13, s32[112,128]{1,0:T(8,128)S(1)} %bitcast.14, f32[1,128]{1,0:T(1,128)S(1)} %bitcast.15), custom_call_target="tpu_custom_call" | custom-call | flops 1000000 | bytes 2000000 | tf_op jit(solution)/shard_map/inner/pallas_call | solution.py:305
  7.8 0.0 collective-permute-done.close_ref
  7.9 0.2 collective-permute-done.1.far_ref
  8.0 0.9 %edge.1 = f32[8,144,128]{2,1,0:T(8,128)} custom-call(f32[8,144,128]{2,1,0:T(8,128)S(1)} %get-tuple-element.12.x_ref, f32[1,8,128]{2,1,0:T(8,128)S(1)} %collective-permute-done.close_ref, f32[1,8,128]{2,1,0:T(8,128)S(1)} %collective-permute-done.1.far_ref), custom_call_target="tpu_custom_call" | custom-call | tf_op jit(solution)/shard_map/edge/pallas_call | solution.py:305
  8.9 5.3 %all-to-all-start = ((f32[8,144,128]{2,1,0:T(8,128)}), f32[8,144,128]{2,1,0:T(8,128)S(1)}, u32[]{:S(2)}, u32[]{:S(2)}) async-start(f32[8,144,128]{2,1,0:T(8,128)} %edge.1), calls=%async_computation | async-start | bytes 1179648 | tf_op jit(solution)/shard_map/all_to_all | solution.py:286
  14.2 0.0 copy-start
  14.2 0.3 gain.1
  14.6 6.4 %collective-permute-start.2 = (f32[8,128]{1,0:T(8,128)S(1)}, f32[8,128]{1,0:T(8,128)S(1)}, u32[]{:S(2)}, u32[]{:S(2)}) collective-permute-start(f32[8,128]{1,0:T(8,128)S(1)} %gain.1), channel_id=1, source_target_pairs={{0,16},{1,17},{2,18},{3,19},{4,20},{5,21},{6,22},{7,23},{8,24},{9,... | collective-permute-start | bytes 12296 | tf_op jit(solution)/shard_map/ppermute | solution.py:290
  20.9 1.6 %collective-permute-done.2 = f32[8,128]{1,0:T(8,128)S(1)} collective-permute-done((f32[8,128]{1,0:T(8,128)S(1)}, f32[8,128]{1,0:T(8,128)S(1)}, u32[]{:S(2)}, u32[]{:S(2)}) %collective-permute-start.2) | collective-permute-done | bytes 4128 | tf_op jit(solution)/shard_map/ppermute | solution.py:290
  22.5 0.0 collective-permute-start.3
  22.5 1.2 %collective-permute-done.3.other_ref = f32[8,128]{1,0:T(8,128)S(1)} collective-permute-done((f32[8,128]{1,0:T(8,128)S(1)}, f32[8,128]{1,0:T(8,128)S(1)}, u32[]{:S(2)}, u32[]{:S(2)}) %collective-permute-start.3) | collective-permute-done | bytes 4128 | tf_op jit(solution)/shard_map/ppermute | solution.py:290
  23.7 1.4 %all-to-all-done.order_ref = f32[8,144,128]{2,1,0:T(8,128)S(1)} async-done(((f32[8,144,128]{2,1,0:T(8,128)}), f32[8,144,128]{2,1,0:T(8,128)S(1)}, u32[]{:S(2)}, u32[]{:S(2)}) %all-to-all-start) | async-done | bytes 589856 | tf_op jit(solution)/shard_map/all_to_all | solution.py:286
  25.1 3.2 %collective-permute-start.4 = (f32[8,128]{1,0:T(8,128)S(1)}, f32[8,128]{1,0:T(8,128)S(1)}, u32[]{:S(2)}, u32[]{:S(2)}) collective-permute-start(f32[8,128]{1,0:T(8,128)S(1)} %add.15.order_ref.gain_ref), channel_id=1, source_target_pairs={{0,2},{1,3},{2,0},{3,1},{4,6},{5,7},{6,4},{7,5},{8,10},{9,11},{10,... | collective-permute-start | bytes 12296 | tf_op jit(solution)/shard_map/ppermute | solution.py:290
  28.3 0.8 %filters.1 = (f32[8,128,128]{2,1,0:T(8,128)S(1)}, f32[8,128,128]{2,1,0:T(8,128)S(1)}, f32[512,128]{1,0:T(8,128)S(1)}) custom-call(f32[1152,128]{1,0:T(8,128)S(1)} %bitcast.11, f32[8,128]{1,0:T(8,128)S(1)} %get-tuple-element.13.aux_ref.order_ref, f32[8,128]{1,0:T(8,128)S(1)} %add.15.order_ref.gain_ref), custom_call_target="tpu_custom_call" | custom-call | flops 100000000 | bytes 4000000 | tf_op jit(solution)/shard_map/filters/pallas_call | solution.py:305
  29.0 0.0 copy-done
  29.0 1.3 %cancel.1.x_ref = f32[256,128]{1,0:T(8,128)S(1)} custom-call(f32[8,128,128]{2,1,0:T(8,128)S(1)} %get-tuple-element.14.v_ref, f32[8,128,128]{2,1,0:T(8,128)S(1)} %get-tuple-element.15.w_ref, f32[512,128]{1,0:T(8,128)S(1)} %get-tuple-element.16.s_ref, f32[14,128,128]{2,1,0:T(8,128)S(1)} %bitcast.12), custom_call_target="tpu_custom_call" | custom-call | flops 100000000 | bytes 4000000 | tf_op jit(solution)/shard_map/cancel/pallas_call | solution.py:305
  30.4 0.0 collective-permute-done.4.other_ref
  30.4 0.7 %pack.1 = (f32[256,128]{1,0:T(8,128)}, f32[8,128]{1,0:T(8,128)S(1)}) custom-call(f32[256,128]{1,0:T(8,128)S(1)} %cancel.1.x_ref, f32[8,128]{1,0:T(8,128)S(1)} %add.15.order_ref.gain_ref, f32[8,128]{1,0:T(8,128)S(1)} %collective-permute-done.4.other_ref), custom_call_target="tpu_custom_call" | custom-call | tf_op jit(solution)/shard_map/pack/pallas_call | solution.py:305
  31.0 0.7 %collective-permute-start.5 = (f32[8,128]{1,0:T(8,128)S(1)}, f32[8,128]{1,0:T(8,128)S(1)}, u32[]{:S(2)}, u32[]{:S(2)}) collective-permute-start(f32[8,128]{1,0:T(8,128)S(1)} %get-tuple-element.18.x_ref), channel_id=1, source_target_pairs={{0,4},{1,5},{2,6},{3,7},{4,0},{5,1},{6,2},{7,3},{8,12},{9,13},{10,... | collective-permute-start | bytes 12296 | tf_op jit(solution)/shard_map/ppermute | solution.py:290
  31.7 5.7 %all-to-all-start.1 = ((f32[8,2,16,128]{3,2,1,0:T(8,128)}), f32[8,2,16,128]{3,2,1,0:T(8,128)S(1)}, u32[]{:S(2)}, u32[]{:S(2)}) async-start(f32[8,2,16,128]{3,2,1,0:T(8,128)} %bitcast.8), calls=%async_computation.1 | async-start | bytes 262144 | tf_op jit(solution)/shard_map/all_to_all | solution.py:286
  37.4 0.0 collective-permute-done.5.other_ref
  37.4 0.9 %collective-permute-start.6 = (f32[8,128]{1,0:T(8,128)S(1)}, f32[8,128]{1,0:T(8,128)S(1)}, u32[]{:S(2)}, u32[]{:S(2)}) collective-permute-start(f32[8,128]{1,0:T(8,128)S(1)} %add.16), channel_id=1, source_target_pairs={{0,8},{1,9},{2,10},{3,11},{4,12},{5,13},{6,14},{7,15},{8,0},{9,1},... | collective-permute-start | bytes 12296 | tf_op jit(solution)/shard_map/ppermute | solution.py:290
  38.3 3.7 %collective-permute-done.6 = f32[8,128]{1,0:T(8,128)S(1)} collective-permute-done((f32[8,128]{1,0:T(8,128)S(1)}, f32[8,128]{1,0:T(8,128)S(1)}, u32[]{:S(2)}, u32[]{:S(2)}) %collective-permute-start.6) | collective-permute-done | bytes 4128 | tf_op jit(solution)/shard_map/ppermute | solution.py:290
  42.0 2.0 %all-to-all-done.1.refs_0_ = f32[8,2,16,128]{3,2,1,0:T(8,128)S(1)} async-done(((f32[8,2,16,128]{3,2,1,0:T(8,128)}), f32[8,2,16,128]{3,2,1,0:T(8,128)S(1)}, u32[]{:S(2)}, u32[]{:S(2)}) %all-to-all-start.1) | async-done | bytes 131104 | tf_op jit(solution)/shard_map/all_to_all | solution.py:286
  44.0 0.9 %finish.1 = f32[14,16,128]{2,1,0:T(8,128)} custom-call(f32[8,2,16,128]{3,2,1,0:T(8,128)S(1)} %all-to-all-done.1.refs_0_, f32[8,128]{1,0:T(8,128)S(1)} %add.14.refs_1_), custom_call_target="tpu_custom_call" | custom-call | tf_op jit(solution)/shard_map/finish/pallas_call | solution.py:305
  (4 shorter events, 0.0 us)
Async XLA Ops:
  0.0 5.5 %copy-start.2 = (s32[128,14,8]{0,2,1:T(8,128)S(1)}, s32[128,14,8]{0,2,1:T(8,128)}, u32[]{:S(2)}) copy-start(s32[128,14,8]{0,2,1:T(8,128)} %param.8) | copy-start | bytes 172036
  0.7 7.1 %collective-permute-start = (f32[1,8,128]{2,1,0:T(8,128)S(1)}, f32[1,8,128]{2,1,0:T(8,128)S(1)}, u32[]{:S(2)}, u32[]{:S(2)}) collective-permute-start(f32[1,8,128]{2,1,0:T(8,128)S(1)} %bitcast.17), channel_id=1, source_target_pairs={{0,1},{1,0},{2,3},{3,2},{4,5},{5,4},{6,7},{7,6},{8,9},{9,8},{10,11... | collective-permute-start | bytes 12296 | tf_op jit(solution)/shard_map/ppermute | solution.py:281
  0.7 7.3 %collective-permute-start.1 = (f32[1,8,128]{2,1,0:T(8,128)S(1)}, f32[1,8,128]{2,1,0:T(8,128)S(1)}, u32[]{:S(2)}, u32[]{:S(2)}) collective-permute-start(f32[1,8,128]{2,1,0:T(8,128)S(1)} %bitcast.16), channel_id=1, source_target_pairs={{1,2},{3,4},{5,6},{7,8},{9,10},{11,12},{13,14},{15,16},{17,18},{19... | collective-permute-start | bytes 12296 | tf_op jit(solution)/shard_map/ppermute | solution.py:280
  5.5 0.7 %copy-start.3 = (s32[16]{0:T(128)S(1)}, s32[16]{0:T(128)}, u32[]{:S(2)}) copy-start(s32[16]{0:T(128)} %seq_ref.1) | copy-start | bytes 196
  5.5 0.7 %copy-start.4 = (f32[128]{0:T(128)S(1)}, f32[128]{0:T(128)}, u32[]{:S(2)}) copy-start(f32[128]{0:T(128)} %param.7) | copy-start | bytes 1540
  6.1 1.0 %copy-start.1 = (f32[128,2,4,128]{3,2,1,0:T(4,128)S(1)}, f32[128,2,4,128]{3,2,1,0:T(4,128)}, u32[]{:S(2)}) copy-start(f32[128,2,4,128]{3,2,1,0:T(4,128)} %param.6) | copy-start | bytes 1572868
  8.9 16.2 %all-to-all-start = ((f32[8,144,128]{2,1,0:T(8,128)}), f32[8,144,128]{2,1,0:T(8,128)S(1)}, u32[]{:S(2)}, u32[]{:S(2)}) async-start(f32[8,144,128]{2,1,0:T(8,128)} %edge.1), calls=%async_computation | async-start | bytes 1179648 | tf_op jit(solution)/shard_map/all_to_all | solution.py:286
  14.2 14.8 %copy-start = (f32[128,14,128]{2,0,1:T(8,128)S(1)}, f32[128,14,128]{2,0,1:T(8,128)}, u32[]{:S(2)}) copy-start(f32[128,14,128]{2,0,1:T(8,128)} %param.5) | copy-start | bytes 2752516
  14.6 8.0 %collective-permute-start.2 = (f32[8,128]{1,0:T(8,128)S(1)}, f32[8,128]{1,0:T(8,128)S(1)}, u32[]{:S(2)}, u32[]{:S(2)}) collective-permute-start(f32[8,128]{1,0:T(8,128)S(1)} %gain.1), channel_id=1, source_target_pairs={{0,16},{1,17},{2,18},{3,19},{4,20},{5,21},{6,22},{7,23},{8,24},{9,... | collective-permute-start | bytes 12296 | tf_op jit(solution)/shard_map/ppermute | solution.py:290
  22.5 1.2 %collective-permute-start.3 = (f32[8,128]{1,0:T(8,128)S(1)}, f32[8,128]{1,0:T(8,128)S(1)}, u32[]{:S(2)}, u32[]{:S(2)}) collective-permute-start(f32[8,128]{1,0:T(8,128)S(1)} %add.13.x_ref), channel_id=1, source_target_pairs={{0,1},{1,0},{2,3},{3,2},{4,5},{5,4},{6,7},{7,6},{8,9},{9,8},{10,11... | collective-permute-start | bytes 12296 | tf_op jit(solution)/shard_map/ppermute | solution.py:290
  25.1 5.3 %collective-permute-start.4 = (f32[8,128]{1,0:T(8,128)S(1)}, f32[8,128]{1,0:T(8,128)S(1)}, u32[]{:S(2)}, u32[]{:S(2)}) collective-permute-start(f32[8,128]{1,0:T(8,128)S(1)} %add.15.order_ref.gain_ref), channel_id=1, source_target_pairs={{0,2},{1,3},{2,0},{3,1},{4,6},{5,7},{6,4},{7,5},{8,10},{9,11},{10,... | collective-permute-start | bytes 12296 | tf_op jit(solution)/shard_map/ppermute | solution.py:290
  31.0 6.4 %collective-permute-start.5 = (f32[8,128]{1,0:T(8,128)S(1)}, f32[8,128]{1,0:T(8,128)S(1)}, u32[]{:S(2)}, u32[]{:S(2)}) collective-permute-start(f32[8,128]{1,0:T(8,128)S(1)} %get-tuple-element.18.x_ref), channel_id=1, source_target_pairs={{0,4},{1,5},{2,6},{3,7},{4,0},{5,1},{6,2},{7,3},{8,12},{9,13},{10,... | collective-permute-start | bytes 12296 | tf_op jit(solution)/shard_map/ppermute | solution.py:290
  31.7 12.3 %all-to-all-start.1 = ((f32[8,2,16,128]{3,2,1,0:T(8,128)}), f32[8,2,16,128]{3,2,1,0:T(8,128)S(1)}, u32[]{:S(2)}, u32[]{:S(2)}) async-start(f32[8,2,16,128]{3,2,1,0:T(8,128)} %bitcast.8), calls=%async_computation.1 | async-start | bytes 262144 | tf_op jit(solution)/shard_map/all_to_all | solution.py:286
  37.4 4.6 %collective-permute-start.6 = (f32[8,128]{1,0:T(8,128)S(1)}, f32[8,128]{1,0:T(8,128)S(1)}, u32[]{:S(2)}, u32[]{:S(2)}) collective-permute-start(f32[8,128]{1,0:T(8,128)S(1)} %add.16), channel_id=1, source_target_pairs={{0,8},{1,9},{2,10},{3,11},{4,12},{5,13},{6,14},{7,15},{8,0},{9,1},... | collective-permute-start | bytes 12296 | tf_op jit(solution)/shard_map/ppermute | solution.py:290

commit v4 on v3

--- a/solution.py
+++ b/solution.py
@@ -287,7 +287,12 @@
 
 
 def from_partner(x, bit):
-    return lax.ppermute(x, "sc", [(i, i ^ bit) for i in range(lax.axis_size("sc"))])
+    code = [z ^ (z >> 1) for z in range(lax.axis_size("sc") // 4)]
+
+    def partner(i):
+        return i ^ bit if bit < 4 else code.index(code[i // 4] ^ (bit // 4)) * 4 + i % 4
+
+    return lax.ppermute(x, "sc", [(i, partner(i)) for i in range(lax.axis_size("sc"))])
 
 
 def kernel(body, shapes, in_specs, name, scratch=(), out_specs=None, aliases=None, flops=0, moved=0):
@@ -321,7 +326,7 @@
     scratch = [pltpu.VMEM(big, F32)]
     gain = kernel(gain_kernel, [tile], [VMEM] * 4, "gain", scratch, flops=10**6, moved=10**6)(near, close, far, aux)
     gain = gain + from_partner(gain, 16)
-    gain = kernel(add_kernel, [tile], [VMEM, VMEM, ANY], "add")(gain, from_partner(gain, 1), gathered)
+    gain = kernel(add_kernel, [tile], [VMEM, VMEM, ANY], "add")(gain, from_partner(gain, 4), gathered)
     scratch = [pltpu.VMEM(big, F32), pltpu.VMEM(big, F32)]
     tiles, filters, symbols = kernel(
         filter_kernel, [big, big, (512, 128)], [VMEM, VMEM, ANY], "filters", scratch, flops=10**8, moved=4 * 10**6
@@ -331,9 +336,9 @@
     estimates = kernel(cancel_kernel, [(256, 128)], [VMEM, VMEM, VMEM, ANY], "cancel", scratch, flops=10**8, moved=4 * 10**6)(
         tiles, filters, symbols, y
     )
-    estimates, gain = kernel(pack_kernel, [(256, 128), tile], [VMEM] * 3, "pack")(estimates, gain, from_partner(gain, 2))
+    estimates, gain = kernel(pack_kernel, [(256, 128), tile], [VMEM] * 3, "pack")(estimates, gain, from_partner(gain, 1))
     estimates = over_sections(estimates.reshape(8, 2, 16, 128))
-    gain = kernel(add_kernel, [tile], [VMEM, VMEM, ANY], "add", flops=10**10, moved=10**8)(gain, from_partner(gain, 4), aux)
+    gain = kernel(add_kernel, [tile], [VMEM, VMEM, ANY], "add", flops=10**10, moved=10**8)(gain, from_partner(gain, 2), aux)
     gain = gain + from_partner(gain, 8)
     count = float(128 * lax.axis_size("sc"))
     body = lambda *refs: finish_kernel(count, *refs)

time: 45.2 us -> 43.4 us (0.960)
  starting transfers between devices: 26.9 us -> 24.4 us
  waiting for transfers between devices: 9.99 us -> 10.6 us
    all_to_all x2, starting transfers between devices: 11 us -> 9.71 us  [over_sections(): return lax.all_to_all(x, 'section', split_axis=0, concat_axis=0, tiled=True)]
    ppermute x5, starting transfers between devices: 11.1 us -> 9.94 us  [from_partner(): lax.ppermute(x, 'sc', [(i, partner(i)) for i in range(lax.axis_size('sc'))])]
    ppermute x5, waiting for transfers between devices: 6.46 us -> 7.59 us  [from_partner(): lax.ppermute(x, 'sc', [(i, partner(i)) for i in range(lax.axis_size('sc'))])]
    all_to_all x2, waiting for transfers between devices: 3.34 us -> 2.87 us  [over_sections(): return lax.all_to_all(x, 'section', split_axis=0, concat_axis=0, tiled=True)]
  transfers between devices with their start and end apart: 9 -> 9, of which waited for: 6 -> 5; matrix products, arithmetic and copies ran while one was open for 0% -> 0% of each run, Pallas kernels for 7% -> 7%
where the time goes in v4:
time: 43.4 us; the launch traced here: 43.1 us
  starting transfers between devices  24.4 us (56%)
  waiting for transfers between devices  10.6 us (24%)
  Pallas kernels  5.5 us (13%)
  local copies, waits for them, and re-layouts  1.7 us (4%)
  other arithmetic  0.72 us (2%)
    ppermute x5, starting transfers between devices, from_partner(): lax.ppermute(x, 'sc', [(i, partner(i)) for i in range(lax.axis_size('sc'))])  9.94 us
    all_to_all x2, starting transfers between devices, over_sections(): return lax.all_to_all(x, 'section', split_axis=0, concat_axis=0, tiled=True)  9.71 us
    ppermute x5, waiting for transfers between devices, from_partner(): lax.ppermute(x, 'sc', [(i, partner(i)) for i in range(lax.axis_size('sc'))])  7.59 us
    pallas_call x9, Pallas kernels, kernel(): return lambda *args: out(*args) if len(shapes) > 1 else out(*args)[0]  5.5 us
    ppermute x1, starting transfers between devices, halo(): far = lax.ppermute(jnp.where(even, h[:1], h[-1:]), 'sc', far)  4.75 us
    all_to_all x2, waiting for transfers between devices, over_sections(): return lax.all_to_all(x, 'section', split_axis=0, concat_axis=0, tiled=True)  2.87 us
    unnamed x10, local copies, waits for them, and re-layouts  1.7 us
  transfers between devices with their start and end apart: 9, of which 5 were waited for; matrix products, arithmetic and copies ran while one was open for 0% of the time, Pallas kernels for 7%

profile of v4, /device:TPU:32, one launch (start us, length us, event | category | flops | bytes accessed | tf_op | source)
XLA Modules:
  0.0 43.1 jit_solution(284237271697358791)
XLA Ops:
  0.0 0.0 copy-start.2
  0.0 0.7 %slice_select_fusion = (f32[1,2,4,128]{3,2,1,0:T(4,128)S(1)}, f32[1,2,4,128]{3,2,1,0:T(4,128)S(1)}) fusion(f32[128,2,4,128]{3,2,1,0:T(4,128)} %param.6, pred[]{:T(512)S(6)} %eq.5), kind=kLoop, calls=%fused_computation | loop fusion | flops 2048 | bytes 16385 | tf_op jit(solution)/shard_map/jit(_where)/select_n | solution.py:280
  0.7 0.0 collective-permute-start
  0.7 4.7 %collective-permute-start.1 = (f32[1,8,128]{2,1,0:T(8,128)S(1)}, f32[1,8,128]{2,1,0:T(8,128)S(1)}, u32[]{:S(2)}, u32[]{:S(2)}) collective-permute-start(f32[1,8,128]{2,1,0:T(8,128)S(1)} %bitcast.16), channel_id=1, source_target_pairs={{1,2},{3,4},{5,6},{7,8},{9,10},{11,12},{13,14},{15,16},{17,18},{19... | collective-permute-start | bytes 12296 | tf_op jit(solution)/shard_map/ppermute | solution.py:280
  5.5 0.0 copy-start.3
  5.5 0.0 copy-start.4
  5.5 0.0 copy-done.2
  5.5 0.6 %copy-done.3 = s32[16]{0:T(128)S(1)} copy-done((s32[16]{0:T(128)S(1)}, s32[16]{0:T(128)}, u32[]{:S(2)}) %copy-start.3) | copy-done | bytes 88
  6.1 0.0 copy-done.4
  6.1 0.0 copy-start.1
  6.2 1.0 %copy-done.1 = f32[128,2,4,128]{3,2,1,0:T(4,128)S(1)} copy-done((f32[128,2,4,128]{3,2,1,0:T(4,128)S(1)}, f32[128,2,4,128]{3,2,1,0:T(4,128)}, u32[]{:S(2)}) %copy-start.1) | copy-done | bytes 524312
  7.2 0.6 %inner.1 = (f32[8,144,128]{2,1,0:T(8,128)S(1)}, f32[8,128]{1,0:T(8,128)S(1)}) custom-call(s32[16]{0:T(128)S(1)} %copy-done.3, f32[128,8,128]{2,1,0:T(8,128)S(1)} %bitcast.13, s32[112,128]{1,0:T(8,128)S(1)} %bitcast.14, f32[1,128]{1,0:T(1,128)S(1)} %bitcast.15), custom_call_target="tpu_custom_call" | custom-call | flops 1000000 | bytes 2000000 | tf_op jit(solution)/shard_map/inner/pallas_call | solution.py:310
  7.8 0.0 collective-permute-done.close_ref
  7.9 0.2 collective-permute-done.1.far_ref
  8.0 0.9 %edge.1 = f32[8,144,128]{2,1,0:T(8,128)} custom-call(f32[8,144,128]{2,1,0:T(8,128)S(1)} %get-tuple-element.12.x_ref, f32[1,8,128]{2,1,0:T(8,128)S(1)} %collective-permute-done.close_ref, f32[1,8,128]{2,1,0:T(8,128)S(1)} %collective-permute-done.1.far_ref), custom_call_target="tpu_custom_call" | custom-call | tf_op jit(solution)/shard_map/edge/pallas_call | solution.py:310
  8.9 5.3 %all-to-all-start = ((f32[8,144,128]{2,1,0:T(8,128)}), f32[8,144,128]{2,1,0:T(8,128)S(1)}, u32[]{:S(2)}, u32[]{:S(2)}) async-start(f32[8,144,128]{2,1,0:T(8,128)} %edge.1), calls=%async_computation | async-start | bytes 1179648 | tf_op jit(solution)/shard_map/all_to_all | solution.py:286
  14.2 0.0 copy-start
  14.2 0.3 gain.1
  14.6 5.9 %collective-permute-start.2 = (f32[8,128]{1,0:T(8,128)S(1)}, f32[8,128]{1,0:T(8,128)S(1)}, u32[]{:S(2)}, u32[]{:S(2)}) collective-permute-start(f32[8,128]{1,0:T(8,128)S(1)} %gain.1), channel_id=1, source_target_pairs={{0,28},{1,29},{2,30},{3,31},{4,24},{5,25},{6,26},{7,27},{8,20},{9,... | collective-permute-start | bytes 12296 | tf_op jit(solution)/shard_map/ppermute | solution.py:295
  20.5 1.6 %collective-permute-done.2 = f32[8,128]{1,0:T(8,128)S(1)} collective-permute-done((f32[8,128]{1,0:T(8,128)S(1)}, f32[8,128]{1,0:T(8,128)S(1)}, u32[]{:S(2)}, u32[]{:S(2)}) %collective-permute-start.2) | collective-permute-done | bytes 4128 | tf_op jit(solution)/shard_map/ppermute | solution.py:295
  22.1 0.1 collective-permute-start.3
  22.2 3.5 %collective-permute-done.3.other_ref = f32[8,128]{1,0:T(8,128)S(1)} collective-permute-done((f32[8,128]{1,0:T(8,128)S(1)}, f32[8,128]{1,0:T(8,128)S(1)}, u32[]{:S(2)}, u32[]{:S(2)}) %collective-permute-start.3) | collective-permute-done | bytes 4128 | tf_op jit(solution)/shard_map/ppermute | solution.py:295
  25.7 0.0 all-to-all-done.order_ref
  25.7 0.0 collective-permute-start.4
  25.7 0.8 %filters.1 = (f32[8,128,128]{2,1,0:T(8,128)S(1)}, f32[8,128,128]{2,1,0:T(8,128)S(1)}, f32[512,128]{1,0:T(8,128)S(1)}) custom-call(f32[1152,128]{1,0:T(8,128)S(1)} %bitcast.11, f32[8,128]{1,0:T(8,128)S(1)} %get-tuple-element.13.aux_ref.order_ref, f32[8,128]{1,0:T(8,128)S(1)} %add.15.order_ref.gain_ref), custom_call_target="tpu_custom_call" | custom-call | flops 100000000 | bytes 4000000 | tf_op jit(solution)/shard_map/filters/pallas_call | solution.py:310
  26.5 0.0 copy-done
  26.5 1.3 %cancel.1.x_ref = f32[256,128]{1,0:T(8,128)S(1)} custom-call(f32[8,128,128]{2,1,0:T(8,128)S(1)} %get-tuple-element.14.v_ref, f32[8,128,128]{2,1,0:T(8,128)S(1)} %get-tuple-element.15.w_ref, f32[512,128]{1,0:T(8,128)S(1)} %get-tuple-element.16.s_ref, f32[14,128,128]{2,1,0:T(8,128)S(1)} %bitcast.12), custom_call_target="tpu_custom_call" | custom-call | flops 100000000 | bytes 4000000 | tf_op jit(solution)/shard_map/cancel/pallas_call | solution.py:310
  27.8 0.0 collective-permute-done.4.other_ref
  27.8 0.7 %pack.1 = (f32[256,128]{1,0:T(8,128)}, f32[8,128]{1,0:T(8,128)S(1)}) custom-call(f32[256,128]{1,0:T(8,128)S(1)} %cancel.1.x_ref, f32[8,128]{1,0:T(8,128)S(1)} %add.15.order_ref.gain_ref, f32[8,128]{1,0:T(8,128)S(1)} %collective-permute-done.4.other_ref), custom_call_target="tpu_custom_call" | custom-call | tf_op jit(solution)/shard_map/pack/pallas_call | solution.py:310
  28.5 2.7 %collective-permute-start.5 = (f32[8,128]{1,0:T(8,128)S(1)}, f32[8,128]{1,0:T(8,128)S(1)}, u32[]{:S(2)}, u32[]{:S(2)}) collective-permute-start(f32[8,128]{1,0:T(8,128)S(1)} %get-tuple-element.18.x_ref), channel_id=1, source_target_pairs={{0,2},{1,3},{2,0},{3,1},{4,6},{5,7},{6,4},{7,5},{8,10},{9,11},{10,... | collective-permute-start | bytes 12296 | tf_op jit(solution)/shard_map/ppermute | solution.py:295
  31.2 4.4 %all-to-all-start.1 = ((f32[8,2,16,128]{3,2,1,0:T(8,128)}), f32[8,2,16,128]{3,2,1,0:T(8,128)S(1)}, u32[]{:S(2)}, u32[]{:S(2)}) async-start(f32[8,2,16,128]{3,2,1,0:T(8,128)} %bitcast.8), calls=%async_computation.1 | async-start | bytes 262144 | tf_op jit(solution)/shard_map/all_to_all | solution.py:286
  35.6 0.0 collective-permute-done.5.other_ref
  35.6 1.2 %collective-permute-start.6 = (f32[8,128]{1,0:T(8,128)S(1)}, f32[8,128]{1,0:T(8,128)S(1)}, u32[]{:S(2)}, u32[]{:S(2)}) collective-permute-start(f32[8,128]{1,0:T(8,128)S(1)} %add.16), channel_id=1, source_target_pairs={{0,12},{1,13},{2,14},{3,15},{4,8},{5,9},{6,10},{7,11},{8,4},{9,5},... | collective-permute-start | bytes 12296 | tf_op jit(solution)/shard_map/ppermute | solution.py:295
  36.8 2.5 %collective-permute-done.6 = f32[8,128]{1,0:T(8,128)S(1)} collective-permute-done((f32[8,128]{1,0:T(8,128)S(1)}, f32[8,128]{1,0:T(8,128)S(1)}, u32[]{:S(2)}, u32[]{:S(2)}) %collective-permute-start.6) | collective-permute-done | bytes 4128 | tf_op jit(solution)/shard_map/ppermute | solution.py:295
  39.3 2.9 %all-to-all-done.1.refs_0_ = f32[8,2,16,128]{3,2,1,0:T(8,128)S(1)} async-done(((f32[8,2,16,128]{3,2,1,0:T(8,128)}), f32[8,2,16,128]{3,2,1,0:T(8,128)S(1)}, u32[]{:S(2)}, u32[]{:S(2)}) %all-to-all-start.1) | async-done | bytes 131104 | tf_op jit(solution)/shard_map/all_to_all | solution.py:286
  42.2 0.9 %finish.1 = f32[14,16,128]{2,1,0:T(8,128)} custom-call(f32[8,2,16,128]{3,2,1,0:T(8,128)S(1)} %all-to-all-done.1.refs_0_, f32[8,128]{1,0:T(8,128)S(1)} %add.14.refs_1_), custom_call_target="tpu_custom_call" | custom-call | tf_op jit(solution)/shard_map/finish/pallas_call | solution.py:310
  (4 shorter events, 0.0 us)
Async XLA Ops:
  0.0 5.5 %copy-start.2 = (s32[128,14,8]{0,2,1:T(8,128)S(1)}, s32[128,14,8]{0,2,1:T(8,128)}, u32[]{:S(2)}) copy-start(s32[128,14,8]{0,2,1:T(8,128)} %param.8) | copy-start | bytes 172036
  0.7 7.1 %collective-permute-start = (f32[1,8,128]{2,1,0:T(8,128)S(1)}, f32[1,8,128]{2,1,0:T(8,128)S(1)}, u32[]{:S(2)}, u32[]{:S(2)}) collective-permute-start(f32[1,8,128]{2,1,0:T(8,128)S(1)} %bitcast.17), channel_id=1, source_target_pairs={{0,1},{1,0},{2,3},{3,2},{4,5},{5,4},{6,7},{7,6},{8,9},{9,8},{10,11... | collective-permute-start | bytes 12296 | tf_op jit(solution)/shard_map/ppermute | solution.py:281
  0.7 7.3 %collective-permute-start.1 = (f32[1,8,128]{2,1,0:T(8,128)S(1)}, f32[1,8,128]{2,1,0:T(8,128)S(1)}, u32[]{:S(2)}, u32[]{:S(2)}) collective-permute-start(f32[1,8,128]{2,1,0:T(8,128)S(1)} %bitcast.16), channel_id=1, source_target_pairs={{1,2},{3,4},{5,6},{7,8},{9,10},{11,12},{13,14},{15,16},{17,18},{19... | collective-permute-start | bytes 12296 | tf_op jit(solution)/shard_map/ppermute | solution.py:280
  5.5 0.7 %copy-start.3 = (s32[16]{0:T(128)S(1)}, s32[16]{0:T(128)}, u32[]{:S(2)}) copy-start(s32[16]{0:T(128)} %seq_ref.1) | copy-start | bytes 196
  5.5 0.7 %copy-start.4 = (f32[128]{0:T(128)S(1)}, f32[128]{0:T(128)}, u32[]{:S(2)}) copy-start(f32[128]{0:T(128)} %param.7) | copy-start | bytes 1540
  6.1 1.0 %copy-start.1 = (f32[128,2,4,128]{3,2,1,0:T(4,128)S(1)}, f32[128,2,4,128]{3,2,1,0:T(4,128)}, u32[]{:S(2)}) copy-start(f32[128,2,4,128]{3,2,1,0:T(4,128)} %param.6) | copy-start | bytes 1572868
  8.9 16.8 %all-to-all-start = ((f32[8,144,128]{2,1,0:T(8,128)}), f32[8,144,128]{2,1,0:T(8,128)S(1)}, u32[]{:S(2)}, u32[]{:S(2)}) async-start(f32[8,144,128]{2,1,0:T(8,128)} %edge.1), calls=%async_computation | async-start | bytes 1179648 | tf_op jit(solution)/shard_map/all_to_all | solution.py:286
  14.2 12.3 %copy-start = (f32[128,14,128]{2,0,1:T(8,128)S(1)}, f32[128,14,128]{2,0,1:T(8,128)}, u32[]{:S(2)}) copy-start(f32[128,14,128]{2,0,1:T(8,128)} %param.5) | copy-start | bytes 2752516
  14.6 7.5 %collective-permute-start.2 = (f32[8,128]{1,0:T(8,128)S(1)}, f32[8,128]{1,0:T(8,128)S(1)}, u32[]{:S(2)}, u32[]{:S(2)}) collective-permute-start(f32[8,128]{1,0:T(8,128)S(1)} %gain.1), channel_id=1, source_target_pairs={{0,28},{1,29},{2,30},{3,31},{4,24},{5,25},{6,26},{7,27},{8,20},{9,... | collective-permute-start | bytes 12296 | tf_op jit(solution)/shard_map/ppermute | solution.py:295
  22.1 3.6 %collective-permute-start.3 = (f32[8,128]{1,0:T(8,128)S(1)}, f32[8,128]{1,0:T(8,128)S(1)}, u32[]{:S(2)}, u32[]{:S(2)}) collective-permute-start(f32[8,128]{1,0:T(8,128)S(1)} %add.13.x_ref), channel_id=1, source_target_pairs={{0,4},{1,5},{2,6},{3,7},{4,0},{5,1},{6,2},{7,3},{8,12},{9,13},{10,... | collective-permute-start | bytes 12296 | tf_op jit(solution)/shard_map/ppermute | solution.py:295
  25.7 2.1 %collective-permute-start.4 = (f32[8,128]{1,0:T(8,128)S(1)}, f32[8,128]{1,0:T(8,128)S(1)}, u32[]{:S(2)}, u32[]{:S(2)}) collective-permute-start(f32[8,128]{1,0:T(8,128)S(1)} %add.15.order_ref.gain_ref), channel_id=1, source_target_pairs={{0,1},{1,0},{2,3},{3,2},{4,5},{5,4},{6,7},{7,6},{8,9},{9,8},{10,11... | collective-permute-start | bytes 12296 | tf_op jit(solution)/shard_map/ppermute | solution.py:295
  28.5 7.1 %collective-permute-start.5 = (f32[8,128]{1,0:T(8,128)S(1)}, f32[8,128]{1,0:T(8,128)S(1)}, u32[]{:S(2)}, u32[]{:S(2)}) collective-permute-start(f32[8,128]{1,0:T(8,128)S(1)} %get-tuple-element.18.x_ref), channel_id=1, source_target_pairs={{0,2},{1,3},{2,0},{3,1},{4,6},{5,7},{6,4},{7,5},{8,10},{9,11},{10,... | collective-permute-start | bytes 12296 | tf_op jit(solution)/shard_map/ppermute | solution.py:295
  31.2 11.0 %all-to-all-start.1 = ((f32[8,2,16,128]{3,2,1,0:T(8,128)}), f32[8,2,16,128]{3,2,1,0:T(8,128)S(1)}, u32[]{:S(2)}, u32[]{:S(2)}) async-start(f32[8,2,16,128]{3,2,1,0:T(8,128)} %bitcast.8), calls=%async_computation.1 | async-start | bytes 262144 | tf_op jit(solution)/shard_map/all_to_all | solution.py:286
  35.6 3.7 %collective-permute-start.6 = (f32[8,128]{1,0:T(8,128)S(1)}, f32[8,128]{1,0:T(8,128)S(1)}, u32[]{:S(2)}, u32[]{:S(2)}) collective-permute-start(f32[8,128]{1,0:T(8,128)S(1)} %add.16), channel_id=1, source_target_pairs={{0,12},{1,13},{2,14},{3,15},{4,8},{5,9},{6,10},{7,11},{8,4},{9,5},... | collective-permute-start | bytes 12296 | tf_op jit(solution)/shard_map/ppermute | solution.py:295

commit v5 on v4

--- a/solution.py
+++ b/solution.py
@@ -112,12 +112,22 @@
     aux_ref[...] = jnp.concatenate([noise, spread, wanted.astype(F32), jnp.zeros((5, 128), F32)], axis=0)
 
 
-def edge_kernel(x_ref, close_ref, far_ref, out_ref):
+def edge_kernel(x_ref, close_ref, far_ref, out_ref, rows_ref, sem_ref):
+    inside = pltpu.make_async_copy(x_ref.at[pl.ds(1, 6)], out_ref.at[pl.ds(1, 6)], sem_ref.at[0])
+    inside.start()
     even = lax.axis_index("sc") % 2 == 0
     close, far = close_ref[0], far_ref[0]
-    out_ref[...] = x_ref[...]
-    out_ref[0, 0:8, :] = x_ref[0, 0:8, :] + 0.25 * jnp.where(even, far, close)
-    out_ref[7, 120:128, :] = x_ref[7, 120:128, :] + 0.25 * jnp.where(even, close, far)
+    rows_ref[0] = x_ref[0]
+    rows_ref[0, 0:8, :] = x_ref[0, 0:8, :] + 0.25 * jnp.where(even, far, close)
+    first = pltpu.make_async_copy(rows_ref.at[0], out_ref.at[0], sem_ref.at[1])
+    first.start()
+    rows_ref[1] = x_ref[7]
+    rows_ref[1, 120:128, :] = x_ref[7, 120:128, :] + 0.25 * jnp.where(even, close, far)
+    last = pltpu.make_async_copy(rows_ref.at[1], out_ref.at[7], sem_ref.at[2])
+    last.start()
+    inside.wait()
+    first.wait()
+    last.wait()
 
 
 def add_kernel(x_ref, other_ref, order_ref, out_ref):
@@ -247,14 +257,15 @@
                     out_ref[pl.ds(half * 16 + g * 8 + c * 4 + u, 8, stride=32), :] = turned[at : at + 8, :]
 
 
-def finish_kernel(count, est_ref, gain_ref, out_ref):
+def finish_kernel(count, est_ref, gain_ref, out_ref, rows_ref, sem_ref):
     total = jnp.sum(gain_ref[...], axis=1, keepdims=True)
     recip = count / total
     block = lax.broadcasted_iota(jnp.int32, (8, 128), 1) // 16
-    for g in range(2):
-        users = [recip[u * 2 + g : u * 2 + g + 1] for u in range(4)]
-        scale = jnp.broadcast_to(jnp.concatenate(users + users, axis=0), (8, 128))
-        for half in range(2):
+    copies = []
+    for half in range(2):
+        for g in range(2):
+            users = [recip[u * 2 + g : u * 2 + g + 1] for u in range(4)]
+            scale = jnp.broadcast_to(jnp.concatenate(users + users, axis=0), (8, 128))
             x = [est_ref[m, half, g * 8 : g * 8 + 8, :] for m in range(8)]
             for bit in (1, 2, 4):
                 low = (block & bit) == 0
@@ -265,10 +276,13 @@
                         new[i] = jnp.where(low, x[i], pltpu.roll(x[j], 16 * bit, 1))
                         new[j] = jnp.where(low, pltpu.roll(x[i], 128 - 16 * bit, 1), x[j])
                 x = new
-            for i in range(8):
-                t = half * 8 + i
-                if t < 14:
-                    out_ref[t, g * 8 : g * 8 + 8, :] = x[i] * scale
+            for i in range(8 - 2 * half):
+                rows_ref[half * 8 + i, g * 8 : g * 8 + 8, :] = x[i] * scale
+        times = pl.ds(half * 8, 8 - 2 * half)
+        copies.append(pltpu.make_async_copy(rows_ref.at[times], out_ref.at[times], sem_ref.at[half]))
+        copies[half].start()
+    for copy in copies:
+        copy.wait()
 
 
 def halo(h):
@@ -322,7 +336,8 @@
     near, aux = kernel(inner_kernel, [rows, tile], [SMEM] + [VMEM] * 3, "inner", flops=10**6, moved=2 * 10**6)(
         detection_sequence, h, labels, noise
     )
-    gathered = over_sections(kernel(edge_kernel, [rows], [VMEM] * 3, "edge")(near, close, far))
+    scratch = [pltpu.VMEM((2, 144, 128), F32), pltpu.SemaphoreType.DMA((3,))]
+    gathered = over_sections(kernel(edge_kernel, [rows], [VMEM] * 3, "edge", scratch, [ANY])(near, close, far))
     scratch = [pltpu.VMEM(big, F32)]
     gain = kernel(gain_kernel, [tile], [VMEM] * 4, "gain", scratch, flops=10**6, moved=10**6)(near, close, far, aux)
     gain = gain + from_partner(gain, 16)
@@ -342,7 +357,7 @@
     gain = gain + from_partner(gain, 8)
     count = float(128 * lax.axis_size("sc"))
     body = lambda *refs: finish_kernel(count, *refs)
-    out = kernel(body, [(14, 16, 128)], [VMEM] * 2, "finish")(estimates, gain)
+    out = kernel(body, [(14, 16, 128)], [VMEM] * 2, "finish", [pltpu.VMEM((14, 16, 128), F32), pltpu.SemaphoreType.DMA((2,))], [ANY])(estimates, gain)
     return out.transpose(2, 0, 1)
 
 

time: 43.4 us -> 43.4 us (level)
  no operation moved by 1% of the time
where the time goes in v5:
time: 43.4 us; the launch traced here: 43.1 us
  starting transfers between devices  24.4 us (56%)
  waiting for transfers between devices  10.6 us (24%)
  Pallas kernels  5.5 us (13%)
  local copies, waits for them, and re-layouts  1.7 us (4%)
  other arithmetic  0.72 us (2%)
    ppermute x5, starting transfers between devices, from_partner(): lax.ppermute(x, 'sc', [(i, partner(i)) for i in range(lax.axis_size('sc'))])  9.91 us
    all_to_all x2, starting transfers between devices, over_sections(): return lax.all_to_all(x, 'section', split_axis=0, concat_axis=0, tiled=True)  9.75 us
    ppermute x5, waiting for transfers between devices, from_partner(): lax.ppermute(x, 'sc', [(i, partner(i)) for i in range(lax.axis_size('sc'))])  7.58 us
    pallas_call x9, Pallas kernels, kernel(): return lambda *args: out(*args) if len(shapes) > 1 else out(*args)[0]  5.5 us
    ppermute x1, starting transfers between devices, halo(): far = lax.ppermute(jnp.where(even, h[:1], h[-1:]), 'sc', far)  4.75 us
    all_to_all x2, waiting for transfers between devices, over_sections(): return lax.all_to_all(x, 'section', split_axis=0, concat_axis=0, tiled=True)  2.87 us
    unnamed x10, local copies, waits for them, and re-layouts  1.7 us
  transfers between devices with their start and end apart: 9, of which 5 were waited for; matrix products, arithmetic and copies ran while one was open for 0% of the time, Pallas kernels for 7%

profile of v5, /device:TPU:32, one launch (start us, length us, event | category | flops | bytes accessed | tf_op | source)
XLA Modules:
  0.0 43.1 jit_solution(1794760758542168435)
XLA Ops:
  0.0 0.0 copy-start.2
  0.0 0.7 %slice_select_fusion = (f32[1,2,4,128]{3,2,1,0:T(4,128)S(1)}, f32[1,2,4,128]{3,2,1,0:T(4,128)S(1)}) fusion(f32[128,2,4,128]{3,2,1,0:T(4,128)} %param.6, pred[]{:T(512)S(6)} %eq.5), kind=kLoop, calls=%fused_computation | loop fusion | flops 2048 | bytes 16385 | tf_op jit(solution)/shard_map/jit(_where)/select_n | solution.py:294
  0.7 0.0 collective-permute-start
  0.7 4.7 %collective-permute-start.1 = (f32[1,8,128]{2,1,0:T(8,128)S(1)}, f32[1,8,128]{2,1,0:T(8,128)S(1)}, u32[]{:S(2)}, u32[]{:S(2)}) collective-permute-start(f32[1,8,128]{2,1,0:T(8,128)S(1)} %bitcast.16), channel_id=1, source_target_pairs={{1,2},{3,4},{5,6},{7,8},{9,10},{11,12},{13,14},{15,16},{17,18},{19... | collective-permute-start | bytes 12296 | tf_op jit(solution)/shard_map/ppermute | solution.py:294
  5.5 0.0 copy-start.3
  5.5 0.0 copy-start.4
  5.5 0.0 copy-done.2
  5.5 0.6 %copy-done.3 = s32[16]{0:T(128)S(1)} copy-done((s32[16]{0:T(128)S(1)}, s32[16]{0:T(128)}, u32[]{:S(2)}) %copy-start.3) | copy-done | bytes 88
  6.1 0.0 copy-done.4
  6.1 0.0 copy-start.1
  6.2 1.0 %copy-done.1 = f32[128,2,4,128]{3,2,1,0:T(4,128)S(1)} copy-done((f32[128,2,4,128]{3,2,1,0:T(4,128)S(1)}, f32[128,2,4,128]{3,2,1,0:T(4,128)}, u32[]{:S(2)}) %copy-start.1) | copy-done | bytes 524312
  7.2 0.6 %inner.1 = (f32[8,144,128]{2,1,0:T(8,128)S(1)}, f32[8,128]{1,0:T(8,128)S(1)}) custom-call(s32[16]{0:T(128)S(1)} %copy-done.3, f32[128,8,128]{2,1,0:T(8,128)S(1)} %bitcast.13, s32[112,128]{1,0:T(8,128)S(1)} %bitcast.14, f32[1,128]{1,0:T(1,128)S(1)} %bitcast.15), custom_call_target="tpu_custom_call" | custom-call | flops 1000000 | bytes 2000000 | tf_op jit(solution)/shard_map/inner/pallas_call | solution.py:324
  7.8 0.0 collective-permute-done.close_ref
  7.9 0.2 collective-permute-done.1.far_ref
  8.0 0.9 %edge.1 = f32[8,144,128]{2,1,0:T(8,128)} custom-call(f32[8,144,128]{2,1,0:T(8,128)S(1)} %get-tuple-element.12.x_ref, f32[1,8,128]{2,1,0:T(8,128)S(1)} %collective-permute-done.close_ref, f32[1,8,128]{2,1,0:T(8,128)S(1)} %collective-permute-done.1.far_ref), custom_call_target="tpu_custom_call" | custom-call | tf_op jit(solution)/shard_map/edge/pallas_call | solution.py:324
  8.9 5.3 %all-to-all-start = ((f32[8,144,128]{2,1,0:T(8,128)}), f32[8,144,128]{2,1,0:T(8,128)S(1)}, u32[]{:S(2)}, u32[]{:S(2)}) async-start(f32[8,144,128]{2,1,0:T(8,128)} %edge.1), calls=%async_computation | async-start | bytes 1179648 | tf_op jit(solution)/shard_map/all_to_all | solution.py:300
  14.2 0.0 copy-start
  14.2 0.3 gain.1
  14.6 5.9 %collective-permute-start.2 = (f32[8,128]{1,0:T(8,128)S(1)}, f32[8,128]{1,0:T(8,128)S(1)}, u32[]{:S(2)}, u32[]{:S(2)}) collective-permute-start(f32[8,128]{1,0:T(8,128)S(1)} %gain.1), channel_id=1, source_target_pairs={{0,28},{1,29},{2,30},{3,31},{4,24},{5,25},{6,26},{7,27},{8,20},{9,... | collective-permute-start | bytes 12296 | tf_op jit(solution)/shard_map/ppermute | solution.py:309
  20.5 1.6 %collective-permute-done.2 = f32[8,128]{1,0:T(8,128)S(1)} collective-permute-done((f32[8,128]{1,0:T(8,128)S(1)}, f32[8,128]{1,0:T(8,128)S(1)}, u32[]{:S(2)}, u32[]{:S(2)}) %collective-permute-start.2) | collective-permute-done | bytes 4128 | tf_op jit(solution)/shard_map/ppermute | solution.py:309
  22.1 0.1 collective-permute-start.3
  22.2 3.5 %collective-permute-done.3.other_ref = f32[8,128]{1,0:T(8,128)S(1)} collective-permute-done((f32[8,128]{1,0:T(8,128)S(1)}, f32[8,128]{1,0:T(8,128)S(1)}, u32[]{:S(2)}, u32[]{:S(2)}) %collective-permute-start.3) | collective-permute-done | bytes 4128 | tf_op jit(solution)/shard_map/ppermute | solution.py:309
  25.7 0.0 all-to-all-done.order_ref
  25.7 0.0 collective-permute-start.4
  25.7 0.8 %filters.1 = (f32[8,128,128]{2,1,0:T(8,128)S(1)}, f32[8,128,128]{2,1,0:T(8,128)S(1)}, f32[512,128]{1,0:T(8,128)S(1)}) custom-call(f32[1152,128]{1,0:T(8,128)S(1)} %bitcast.11, f32[8,128]{1,0:T(8,128)S(1)} %get-tuple-element.13.aux_ref.order_ref, f32[8,128]{1,0:T(8,128)S(1)} %add.15.order_ref.gain_ref), custom_call_target="tpu_custom_call" | custom-call | flops 100000000 | bytes 4000000 | tf_op jit(solution)/shard_map/filters/pallas_call | solution.py:324
  26.5 0.0 copy-done
  26.5 1.3 %cancel.1.x_ref = f32[256,128]{1,0:T(8,128)S(1)} custom-call(f32[8,128,128]{2,1,0:T(8,128)S(1)} %get-tuple-element.14.v_ref, f32[8,128,128]{2,1,0:T(8,128)S(1)} %get-tuple-element.15.w_ref, f32[512,128]{1,0:T(8,128)S(1)} %get-tuple-element.16.s_ref, f32[14,128,128]{2,1,0:T(8,128)S(1)} %bitcast.12), custom_call_target="tpu_custom_call" | custom-call | flops 100000000 | bytes 4000000 | tf_op jit(solution)/shard_map/cancel/pallas_call | solution.py:324
  27.8 0.0 collective-permute-done.4.other_ref
  27.8 0.7 %pack.1 = (f32[256,128]{1,0:T(8,128)}, f32[8,128]{1,0:T(8,128)S(1)}) custom-call(f32[256,128]{1,0:T(8,128)S(1)} %cancel.1.x_ref, f32[8,128]{1,0:T(8,128)S(1)} %add.15.order_ref.gain_ref, f32[8,128]{1,0:T(8,128)S(1)} %collective-permute-done.4.other_ref), custom_call_target="tpu_custom_call" | custom-call | tf_op jit(solution)/shard_map/pack/pallas_call | solution.py:324
  28.5 2.7 %collective-permute-start.5 = (f32[8,128]{1,0:T(8,128)S(1)}, f32[8,128]{1,0:T(8,128)S(1)}, u32[]{:S(2)}, u32[]{:S(2)}) collective-permute-start(f32[8,128]{1,0:T(8,128)S(1)} %get-tuple-element.18.x_ref), channel_id=1, source_target_pairs={{0,2},{1,3},{2,0},{3,1},{4,6},{5,7},{6,4},{7,5},{8,10},{9,11},{10,... | collective-permute-start | bytes 12296 | tf_op jit(solution)/shard_map/ppermute | solution.py:309
  31.2 4.4 %all-to-all-start.1 = ((f32[8,2,16,128]{3,2,1,0:T(8,128)}), f32[8,2,16,128]{3,2,1,0:T(8,128)S(1)}, u32[]{:S(2)}, u32[]{:S(2)}) async-start(f32[8,2,16,128]{3,2,1,0:T(8,128)} %bitcast.8), calls=%async_computation.1 | async-start | bytes 262144 | tf_op jit(solution)/shard_map/all_to_all | solution.py:300
  35.6 0.0 collective-permute-done.5.other_ref
  35.6 1.2 %collective-permute-start.6 = (f32[8,128]{1,0:T(8,128)S(1)}, f32[8,128]{1,0:T(8,128)S(1)}, u32[]{:S(2)}, u32[]{:S(2)}) collective-permute-start(f32[8,128]{1,0:T(8,128)S(1)} %add.16), channel_id=1, source_target_pairs={{0,12},{1,13},{2,14},{3,15},{4,8},{5,9},{6,10},{7,11},{8,4},{9,5},... | collective-permute-start | bytes 12296 | tf_op jit(solution)/shard_map/ppermute | solution.py:309
  36.8 2.5 %collective-permute-done.6 = f32[8,128]{1,0:T(8,128)S(1)} collective-permute-done((f32[8,128]{1,0:T(8,128)S(1)}, f32[8,128]{1,0:T(8,128)S(1)}, u32[]{:S(2)}, u32[]{:S(2)}) %collective-permute-start.6) | collective-permute-done | bytes 4128 | tf_op jit(solution)/shard_map/ppermute | solution.py:309
  39.3 2.9 %all-to-all-done.1.refs_0_ = f32[8,2,16,128]{3,2,1,0:T(8,128)S(1)} async-done(((f32[8,2,16,128]{3,2,1,0:T(8,128)}), f32[8,2,16,128]{3,2,1,0:T(8,128)S(1)}, u32[]{:S(2)}, u32[]{:S(2)}) %all-to-all-start.1) | async-done | bytes 131104 | tf_op jit(solution)/shard_map/all_to_all | solution.py:300
  42.2 0.9 %finish.1 = f32[14,16,128]{2,1,0:T(8,128)} custom-call(f32[8,2,16,128]{3,2,1,0:T(8,128)S(1)} %all-to-all-done.1.refs_0_, f32[8,128]{1,0:T(8,128)S(1)} %add.14.refs_1_), custom_call_target="tpu_custom_call" | custom-call | tf_op jit(solution)/shard_map/finish/pallas_call | solution.py:324
  (4 shorter events, 0.0 us)
Async XLA Ops:
  0.0 5.5 %copy-start.2 = (s32[128,14,8]{0,2,1:T(8,128)S(1)}, s32[128,14,8]{0,2,1:T(8,128)}, u32[]{:S(2)}) copy-start(s32[128,14,8]{0,2,1:T(8,128)} %param.8) | copy-start | bytes 172036
  0.7 7.1 %collective-permute-start = (f32[1,8,128]{2,1,0:T(8,128)S(1)}, f32[1,8,128]{2,1,0:T(8,128)S(1)}, u32[]{:S(2)}, u32[]{:S(2)}) collective-permute-start(f32[1,8,128]{2,1,0:T(8,128)S(1)} %bitcast.17), channel_id=1, source_target_pairs={{0,1},{1,0},{2,3},{3,2},{4,5},{5,4},{6,7},{7,6},{8,9},{9,8},{10,11... | collective-permute-start | bytes 12296 | tf_op jit(solution)/shard_map/ppermute | solution.py:295
  0.7 7.3 %collective-permute-start.1 = (f32[1,8,128]{2,1,0:T(8,128)S(1)}, f32[1,8,128]{2,1,0:T(8,128)S(1)}, u32[]{:S(2)}, u32[]{:S(2)}) collective-permute-start(f32[1,8,128]{2,1,0:T(8,128)S(1)} %bitcast.16), channel_id=1, source_target_pairs={{1,2},{3,4},{5,6},{7,8},{9,10},{11,12},{13,14},{15,16},{17,18},{19... | collective-permute-start | bytes 12296 | tf_op jit(solution)/shard_map/ppermute | solution.py:294
  5.5 0.7 %copy-start.3 = (s32[16]{0:T(128)S(1)}, s32[16]{0:T(128)}, u32[]{:S(2)}) copy-start(s32[16]{0:T(128)} %seq_ref.1) | copy-start | bytes 196
  5.5 0.7 %copy-start.4 = (f32[128]{0:T(128)S(1)}, f32[128]{0:T(128)}, u32[]{:S(2)}) copy-start(f32[128]{0:T(128)} %param.7) | copy-start | bytes 1540
  6.1 1.0 %copy-start.1 = (f32[128,2,4,128]{3,2,1,0:T(4,128)S(1)}, f32[128,2,4,128]{3,2,1,0:T(4,128)}, u32[]{:S(2)}) copy-start(f32[128,2,4,128]{3,2,1,0:T(4,128)} %param.6) | copy-start | bytes 1572868
  8.9 16.8 %all-to-all-start = ((f32[8,144,128]{2,1,0:T(8,128)}), f32[8,144,128]{2,1,0:T(8,128)S(1)}, u32[]{:S(2)}, u32[]{:S(2)}) async-start(f32[8,144,128]{2,1,0:T(8,128)} %edge.1), calls=%async_computation | async-start | bytes 1179648 | tf_op jit(solution)/shard_map/all_to_all | solution.py:300
  14.2 12.3 %copy-start = (f32[128,14,128]{2,0,1:T(8,128)S(1)}, f32[128,14,128]{2,0,1:T(8,128)}, u32[]{:S(2)}) copy-start(f32[128,14,128]{2,0,1:T(8,128)} %param.5) | copy-start | bytes 2752516
  14.6 7.5 %collective-permute-start.2 = (f32[8,128]{1,0:T(8,128)S(1)}, f32[8,128]{1,0:T(8,128)S(1)}, u32[]{:S(2)}, u32[]{:S(2)}) collective-permute-start(f32[8,128]{1,0:T(8,128)S(1)} %gain.1), channel_id=1, source_target_pairs={{0,28},{1,29},{2,30},{3,31},{4,24},{5,25},{6,26},{7,27},{8,20},{9,... | collective-permute-start | bytes 12296 | tf_op jit(solution)/shard_map/ppermute | solution.py:309
  22.1 3.6 %collective-permute-start.3 = (f32[8,128]{1,0:T(8,128)S(1)}, f32[8,128]{1,0:T(8,128)S(1)}, u32[]{:S(2)}, u32[]{:S(2)}) collective-permute-start(f32[8,128]{1,0:T(8,128)S(1)} %add.13.x_ref), channel_id=1, source_target_pairs={{0,4},{1,5},{2,6},{3,7},{4,0},{5,1},{6,2},{7,3},{8,12},{9,13},{10,... | collective-permute-start | bytes 12296 | tf_op jit(solution)/shard_map/ppermute | solution.py:309
  25.7 2.1 %collective-permute-start.4 = (f32[8,128]{1,0:T(8,128)S(1)}, f32[8,128]{1,0:T(8,128)S(1)}, u32[]{:S(2)}, u32[]{:S(2)}) collective-permute-start(f32[8,128]{1,0:T(8,128)S(1)} %add.15.order_ref.gain_ref), channel_id=1, source_target_pairs={{0,1},{1,0},{2,3},{3,2},{4,5},{5,4},{6,7},{7,6},{8,9},{9,8},{10,11... | collective-permute-start | bytes 12296 | tf_op jit(solution)/shard_map/ppermute | solution.py:309
  28.5 7.1 %collective-permute-start.5 = (f32[8,128]{1,0:T(8,128)S(1)}, f32[8,128]{1,0:T(8,128)S(1)}, u32[]{:S(2)}, u32[]{:S(2)}) collective-permute-start(f32[8,128]{1,0:T(8,128)S(1)} %get-tuple-element.18.x_ref), channel_id=1, source_target_pairs={{0,2},{1,3},{2,0},{3,1},{4,6},{5,7},{6,4},{7,5},{8,10},{9,11},{10,... | collective-permute-start | bytes 12296 | tf_op jit(solution)/shard_map/ppermute | solution.py:309
  31.2 11.0 %all-to-all-start.1 = ((f32[8,2,16,128]{3,2,1,0:T(8,128)}), f32[8,2,16,128]{3,2,1,0:T(8,128)S(1)}, u32[]{:S(2)}, u32[]{:S(2)}) async-start(f32[8,2,16,128]{3,2,1,0:T(8,128)} %bitcast.8), calls=%async_computation.1 | async-start | bytes 262144 | tf_op jit(solution)/shard_map/all_to_all | solution.py:300
  35.6 3.7 %collective-permute-start.6 = (f32[8,128]{1,0:T(8,128)S(1)}, f32[8,128]{1,0:T(8,128)S(1)}, u32[]{:S(2)}, u32[]{:S(2)}) collective-permute-start(f32[8,128]{1,0:T(8,128)S(1)} %add.16), channel_id=1, source_target_pairs={{0,12},{1,13},{2,14},{3,15},{4,8},{5,9},{6,10},{7,11},{8,4},{9,5},... | collective-permute-start | bytes 12296 | tf_op jit(solution)/shard_map/ppermute | solution.py:309

commit v6 on v5

--- a/solution.py
+++ b/solution.py
@@ -156,7 +156,7 @@
     out_ref[...] = jnp.concatenate([1.0 - noise * p[u, u] for u in range(4)], axis=0)
 
 
-def filter_kernel(x_ref, aux_ref, order_ref, v_ref, w_ref, s_ref, t_ref, f_ref):
+def filter_kernel(x_ref, aux_ref, v_ref, w_ref, s_ref, t_ref, f_ref):
     for i in range(8):
         for f in range(16):
             v_ref[i, f * 8 : f * 8 + 8, :] = x_ref[pl.ds(f * 8 + i, 8, stride=144), :]
@@ -344,8 +344,8 @@
     gain = kernel(add_kernel, [tile], [VMEM, VMEM, ANY], "add")(gain, from_partner(gain, 4), gathered)
     scratch = [pltpu.VMEM(big, F32), pltpu.VMEM(big, F32)]
     tiles, filters, symbols = kernel(
-        filter_kernel, [big, big, (512, 128)], [VMEM, VMEM, ANY], "filters", scratch, flops=10**8, moved=4 * 10**6
-    )(gathered.reshape(1152, 128), aux, gain)
+        filter_kernel, [big, big, (512, 128)], [VMEM, VMEM], "filters", scratch, flops=10**8, moved=4 * 10**6
+    )(gathered.reshape(1152, 128), aux)
     scratch = [pltpu.VMEM((16, 16, 128), F32), pltpu.VMEM((256, 128), F32), pltpu.VMEM((256, 128), F32)]
     scratch += [pltpu.VMEM((16, 80, 128), F32), pltpu.SemaphoreType.DMA]
     estimates = kernel(cancel_kernel, [(256, 128)], [VMEM, VMEM, VMEM, ANY], "cancel", scratch, flops=10**8, moved=4 * 10**6)(

time: 43.4 us -> 43.4 us (level)
  no operation moved by 1% of the time
where the time goes in v6:
time: 43.4 us; the launch traced here: 43.1 us
  starting transfers between devices  24.4 us (56%)
  waiting for transfers between devices  10.6 us (24%)
  Pallas kernels  5.5 us (13%)
  local copies, waits for them, and re-layouts  1.7 us (4%)
  other arithmetic  0.72 us (2%)
    ppermute x5, starting transfers between devices, from_partner(): lax.ppermute(x, 'sc', [(i, partner(i)) for i in range(lax.axis_size('sc'))])  9.91 us
    all_to_all x2, starting transfers between devices, over_sections(): return lax.all_to_all(x, 'section', split_axis=0, concat_axis=0, tiled=True)  9.75 us
    ppermute x5, waiting for transfers between devices, from_partner(): lax.ppermute(x, 'sc', [(i, partner(i)) for i in range(lax.axis_size('sc'))])  7.59 us
    pallas_call x9, Pallas kernels, kernel(): return lambda *args: out(*args) if len(shapes) > 1 else out(*args)[0]  5.5 us
    ppermute x1, starting transfers between devices, halo(): far = lax.ppermute(jnp.where(even, h[:1], h[-1:]), 'sc', far)  4.75 us
    all_to_all x2, waiting for transfers between devices, over_sections(): return lax.all_to_all(x, 'section', split_axis=0, concat_axis=0, tiled=True)  2.87 us
    unnamed x10, local copies, waits for them, and re-layouts  1.7 us
  transfers between devices with their start and end apart: 9, of which 5 were waited for; matrix products, arithmetic and copies ran while one was open for 0% of the time, Pallas kernels for 7%

profile of v6, /device:TPU:32, one launch (start us, length us, event | category | flops | bytes accessed | tf_op | source)
XLA Modules:
  0.0 43.1 jit_solution(11767040544697754236)
XLA Ops:
  0.0 0.0 copy-start.2
  0.0 0.7 %slice_select_fusion = (f32[1,2,4,128]{3,2,1,0:T(4,128)S(1)}, f32[1,2,4,128]{3,2,1,0:T(4,128)S(1)}) fusion(f32[128,2,4,128]{3,2,1,0:T(4,128)} %param.6, pred[]{:T(512)S(6)} %eq.5), kind=kLoop, calls=%fused_computation | loop fusion | flops 2048 | bytes 16385 | tf_op jit(solution)/shard_map/jit(_where)/select_n | solution.py:294
  0.7 0.0 collective-permute-start
  0.7 4.7 %collective-permute-start.1 = (f32[1,8,128]{2,1,0:T(8,128)S(1)}, f32[1,8,128]{2,1,0:T(8,128)S(1)}, u32[]{:S(2)}, u32[]{:S(2)}) collective-permute-start(f32[1,8,128]{2,1,0:T(8,128)S(1)} %bitcast.16), channel_id=1, source_target_pairs={{1,2},{3,4},{5,6},{7,8},{9,10},{11,12},{13,14},{15,16},{17,18},{19... | collective-permute-start | bytes 12296 | tf_op jit(solution)/shard_map/ppermute | solution.py:294
  5.5 0.0 copy-start.3
  5.5 0.0 copy-start.4
  5.5 0.0 copy-done.2
  5.5 0.6 %copy-done.3 = s32[16]{0:T(128)S(1)} copy-done((s32[16]{0:T(128)S(1)}, s32[16]{0:T(128)}, u32[]{:S(2)}) %copy-start.3) | copy-done | bytes 88
  6.1 0.0 copy-done.4
  6.1 0.0 copy-start.1
  6.2 1.0 %copy-done.1 = f32[128,2,4,128]{3,2,1,0:T(4,128)S(1)} copy-done((f32[128,2,4,128]{3,2,1,0:T(4,128)S(1)}, f32[128,2,4,128]{3,2,1,0:T(4,128)}, u32[]{:S(2)}) %copy-start.1) | copy-done | bytes 524312
  7.2 0.6 %inner.1 = (f32[8,144,128]{2,1,0:T(8,128)S(1)}, f32[8,128]{1,0:T(8,128)S(1)}) custom-call(s32[16]{0:T(128)S(1)} %copy-done.3, f32[128,8,128]{2,1,0:T(8,128)S(1)} %bitcast.13, s32[112,128]{1,0:T(8,128)S(1)} %bitcast.14, f32[1,128]{1,0:T(1,128)S(1)} %bitcast.15), custom_call_target="tpu_custom_call" | custom-call | flops 1000000 | bytes 2000000 | tf_op jit(solution)/shard_map/inner/pallas_call | solution.py:324
  7.8 0.0 collective-permute-done.close_ref
  7.9 0.2 collective-permute-done.1.far_ref
  8.0 0.9 %edge.1 = f32[8,144,128]{2,1,0:T(8,128)} custom-call(f32[8,144,128]{2,1,0:T(8,128)S(1)} %get-tuple-element.12.x_ref, f32[1,8,128]{2,1,0:T(8,128)S(1)} %collective-permute-done.close_ref, f32[1,8,128]{2,1,0:T(8,128)S(1)} %collective-permute-done.1.far_ref), custom_call_target="tpu_custom_call" | custom-call | tf_op jit(solution)/shard_map/edge/pallas_call | solution.py:324
  8.9 5.3 %all-to-all-start = ((f32[8,144,128]{2,1,0:T(8,128)}), f32[8,144,128]{2,1,0:T(8,128)S(1)}, u32[]{:S(2)}, u32[]{:S(2)}) async-start(f32[8,144,128]{2,1,0:T(8,128)} %edge.1), calls=%async_computation | async-start | bytes 1179648 | tf_op jit(solution)/shard_map/all_to_all | solution.py:300
  14.2 0.0 copy-start
  14.2 0.3 gain.1
  14.6 5.9 %collective-permute-start.2 = (f32[8,128]{1,0:T(8,128)S(1)}, f32[8,128]{1,0:T(8,128)S(1)}, u32[]{:S(2)}, u32[]{:S(2)}) collective-permute-start(f32[8,128]{1,0:T(8,128)S(1)} %gain.1), channel_id=1, source_target_pairs={{0,28},{1,29},{2,30},{3,31},{4,24},{5,25},{6,26},{7,27},{8,20},{9,... | collective-permute-start | bytes 12296 | tf_op jit(solution)/shard_map/ppermute | solution.py:309
  20.5 1.6 %collective-permute-done.2 = f32[8,128]{1,0:T(8,128)S(1)} collective-permute-done((f32[8,128]{1,0:T(8,128)S(1)}, f32[8,128]{1,0:T(8,128)S(1)}, u32[]{:S(2)}, u32[]{:S(2)}) %collective-permute-start.2) | collective-permute-done | bytes 4128 | tf_op jit(solution)/shard_map/ppermute | solution.py:309
  22.1 0.1 collective-permute-start.3
  22.2 3.5 %collective-permute-done.3.other_ref = f32[8,128]{1,0:T(8,128)S(1)} collective-permute-done((f32[8,128]{1,0:T(8,128)S(1)}, f32[8,128]{1,0:T(8,128)S(1)}, u32[]{:S(2)}, u32[]{:S(2)}) %collective-permute-start.3) | collective-permute-done | bytes 4128 | tf_op jit(solution)/shard_map/ppermute | solution.py:309
  25.7 0.0 all-to-all-done.order_ref
  25.7 0.0 collective-permute-start.4
  25.7 0.8 %filters.1 = (f32[8,128,128]{2,1,0:T(8,128)S(1)}, f32[8,128,128]{2,1,0:T(8,128)S(1)}, f32[512,128]{1,0:T(8,128)S(1)}) custom-call(f32[1152,128]{1,0:T(8,128)S(1)} %bitcast.11, f32[8,128]{1,0:T(8,128)S(1)} %get-tuple-element.13.aux_ref.order_ref), custom_call_target="tpu_custom_call" | custom-call | flops 100000000 | bytes 4000000 | tf_op jit(solution)/shard_map/filters/pallas_call | solution.py:324
  26.5 0.0 copy-done
  26.5 1.3 %cancel.1.x_ref = f32[256,128]{1,0:T(8,128)S(1)} custom-call(f32[8,128,128]{2,1,0:T(8,128)S(1)} %get-tuple-element.14.v_ref, f32[8,128,128]{2,1,0:T(8,128)S(1)} %get-tuple-element.15.w_ref, f32[512,128]{1,0:T(8,128)S(1)} %get-tuple-element.16.s_ref, f32[14,128,128]{2,1,0:T(8,128)S(1)} %bitcast.12), custom_call_target="tpu_custom_call" | custom-call | flops 100000000 | bytes 4000000 | tf_op jit(solution)/shard_map/cancel/pallas_call | solution.py:324
  27.8 0.0 collective-permute-done.4.other_ref
  27.8 0.7 %pack.1 = (f32[256,128]{1,0:T(8,128)}, f32[8,128]{1,0:T(8,128)S(1)}) custom-call(f32[256,128]{1,0:T(8,128)S(1)} %cancel.1.x_ref, f32[8,128]{1,0:T(8,128)S(1)} %add.15.gain_ref, f32[8,128]{1,0:T(8,128)S(1)} %collective-permute-done.4.other_ref), custom_call_target="tpu_custom_call" | custom-call | tf_op jit(solution)/shard_map/pack/pallas_call | solution.py:324
  28.5 2.7 %collective-permute-start.5 = (f32[8,128]{1,0:T(8,128)S(1)}, f32[8,128]{1,0:T(8,128)S(1)}, u32[]{:S(2)}, u32[]{:S(2)}) collective-permute-start(f32[8,128]{1,0:T(8,128)S(1)} %get-tuple-element.18.x_ref), channel_id=1, source_target_pairs={{0,2},{1,3},{2,0},{3,1},{4,6},{5,7},{6,4},{7,5},{8,10},{9,11},{10,... | collective-permute-start | bytes 12296 | tf_op jit(solution)/shard_map/ppermute | solution.py:309
  31.2 4.4 %all-to-all-start.1 = ((f32[8,2,16,128]{3,2,1,0:T(8,128)}), f32[8,2,16,128]{3,2,1,0:T(8,128)S(1)}, u32[]{:S(2)}, u32[]{:S(2)}) async-start(f32[8,2,16,128]{3,2,1,0:T(8,128)} %bitcast.8), calls=%async_computation.1 | async-start | bytes 262144 | tf_op jit(solution)/shard_map/all_to_all | solution.py:300
  35.6 0.0 collective-permute-done.5.other_ref
  35.6 1.2 %collective-permute-start.6 = (f32[8,128]{1,0:T(8,128)S(1)}, f32[8,128]{1,0:T(8,128)S(1)}, u32[]{:S(2)}, u32[]{:S(2)}) collective-permute-start(f32[8,128]{1,0:T(8,128)S(1)} %add.16), channel_id=1, source_target_pairs={{0,12},{1,13},{2,14},{3,15},{4,8},{5,9},{6,10},{7,11},{8,4},{9,5},... | collective-permute-start | bytes 12296 | tf_op jit(solution)/shard_map/ppermute | solution.py:309
  36.8 2.5 %collective-permute-done.6 = f32[8,128]{1,0:T(8,128)S(1)} collective-permute-done((f32[8,128]{1,0:T(8,128)S(1)}, f32[8,128]{1,0:T(8,128)S(1)}, u32[]{:S(2)}, u32[]{:S(2)}) %collective-permute-start.6) | collective-permute-done | bytes 4128 | tf_op jit(solution)/shard_map/ppermute | solution.py:309
  39.3 2.9 %all-to-all-done.1.refs_0_ = f32[8,2,16,128]{3,2,1,0:T(8,128)S(1)} async-done(((f32[8,2,16,128]{3,2,1,0:T(8,128)}), f32[8,2,16,128]{3,2,1,0:T(8,128)S(1)}, u32[]{:S(2)}, u32[]{:S(2)}) %all-to-all-start.1) | async-done | bytes 131104 | tf_op jit(solution)/shard_map/all_to_all | solution.py:300
  42.2 0.9 %finish.1 = f32[14,16,128]{2,1,0:T(8,128)} custom-call(f32[8,2,16,128]{3,2,1,0:T(8,128)S(1)} %all-to-all-done.1.refs_0_, f32[8,128]{1,0:T(8,128)S(1)} %add.14.refs_1_), custom_call_target="tpu_custom_call" | custom-call | tf_op jit(solution)/shard_map/finish/pallas_call | solution.py:324
  (4 shorter events, 0.0 us)
Async XLA Ops:
  0.0 5.5 %copy-start.2 = (s32[128,14,8]{0,2,1:T(8,128)S(1)}, s32[128,14,8]{0,2,1:T(8,128)}, u32[]{:S(2)}) copy-start(s32[128,14,8]{0,2,1:T(8,128)} %param.8) | copy-start | bytes 172036
  0.7 7.1 %collective-permute-start = (f32[1,8,128]{2,1,0:T(8,128)S(1)}, f32[1,8,128]{2,1,0:T(8,128)S(1)}, u32[]{:S(2)}, u32[]{:S(2)}) collective-permute-start(f32[1,8,128]{2,1,0:T(8,128)S(1)} %bitcast.17), channel_id=1, source_target_pairs={{0,1},{1,0},{2,3},{3,2},{4,5},{5,4},{6,7},{7,6},{8,9},{9,8},{10,11... | collective-permute-start | bytes 12296 | tf_op jit(solution)/shard_map/ppermute | solution.py:295
  0.7 7.3 %collective-permute-start.1 = (f32[1,8,128]{2,1,0:T(8,128)S(1)}, f32[1,8,128]{2,1,0:T(8,128)S(1)}, u32[]{:S(2)}, u32[]{:S(2)}) collective-permute-start(f32[1,8,128]{2,1,0:T(8,128)S(1)} %bitcast.16), channel_id=1, source_target_pairs={{1,2},{3,4},{5,6},{7,8},{9,10},{11,12},{13,14},{15,16},{17,18},{19... | collective-permute-start | bytes 12296 | tf_op jit(solution)/shard_map/ppermute | solution.py:294
  5.5 0.7 %copy-start.3 = (s32[16]{0:T(128)S(1)}, s32[16]{0:T(128)}, u32[]{:S(2)}) copy-start(s32[16]{0:T(128)} %seq_ref.1) | copy-start | bytes 196
  5.5 0.7 %copy-start.4 = (f32[128]{0:T(128)S(1)}, f32[128]{0:T(128)}, u32[]{:S(2)}) copy-start(f32[128]{0:T(128)} %param.7) | copy-start | bytes 1540
  6.1 1.0 %copy-start.1 = (f32[128,2,4,128]{3,2,1,0:T(4,128)S(1)}, f32[128,2,4,128]{3,2,1,0:T(4,128)}, u32[]{:S(2)}) copy-start(f32[128,2,4,128]{3,2,1,0:T(4,128)} %param.6) | copy-start | bytes 1572868
  8.9 16.8 %all-to-all-start = ((f32[8,144,128]{2,1,0:T(8,128)}), f32[8,144,128]{2,1,0:T(8,128)S(1)}, u32[]{:S(2)}, u32[]{:S(2)}) async-start(f32[8,144,128]{2,1,0:T(8,128)} %edge.1), calls=%async_computation | async-start | bytes 1179648 | tf_op jit(solution)/shard_map/all_to_all | solution.py:300
  14.2 12.3 %copy-start = (f32[128,14,128]{2,0,1:T(8,128)S(1)}, f32[128,14,128]{2,0,1:T(8,128)}, u32[]{:S(2)}) copy-start(f32[128,14,128]{2,0,1:T(8,128)} %param.5) | copy-start | bytes 2752516
  14.6 7.5 %collective-permute-start.2 = (f32[8,128]{1,0:T(8,128)S(1)}, f32[8,128]{1,0:T(8,128)S(1)}, u32[]{:S(2)}, u32[]{:S(2)}) collective-permute-start(f32[8,128]{1,0:T(8,128)S(1)} %gain.1), channel_id=1, source_target_pairs={{0,28},{1,29},{2,30},{3,31},{4,24},{5,25},{6,26},{7,27},{8,20},{9,... | collective-permute-start | bytes 12296 | tf_op jit(solution)/shard_map/ppermute | solution.py:309
  22.1 3.6 %collective-permute-start.3 = (f32[8,128]{1,0:T(8,128)S(1)}, f32[8,128]{1,0:T(8,128)S(1)}, u32[]{:S(2)}, u32[]{:S(2)}) collective-permute-start(f32[8,128]{1,0:T(8,128)S(1)} %add.13.x_ref), channel_id=1, source_target_pairs={{0,4},{1,5},{2,6},{3,7},{4,0},{5,1},{6,2},{7,3},{8,12},{9,13},{10,... | collective-permute-start | bytes 12296 | tf_op jit(solution)/shard_map/ppermute | solution.py:309
  25.7 2.1 %collective-permute-start.4 = (f32[8,128]{1,0:T(8,128)S(1)}, f32[8,128]{1,0:T(8,128)S(1)}, u32[]{:S(2)}, u32[]{:S(2)}) collective-permute-start(f32[8,128]{1,0:T(8,128)S(1)} %add.15.gain_ref), channel_id=1, source_target_pairs={{0,1},{1,0},{2,3},{3,2},{4,5},{5,4},{6,7},{7,6},{8,9},{9,8},{10,11... | collective-permute-start | bytes 12296 | tf_op jit(solution)/shard_map/ppermute | solution.py:309
  28.5 7.1 %collective-permute-start.5 = (f32[8,128]{1,0:T(8,128)S(1)}, f32[8,128]{1,0:T(8,128)S(1)}, u32[]{:S(2)}, u32[]{:S(2)}) collective-permute-start(f32[8,128]{1,0:T(8,128)S(1)} %get-tuple-element.18.x_ref), channel_id=1, source_target_pairs={{0,2},{1,3},{2,0},{3,1},{4,6},{5,7},{6,4},{7,5},{8,10},{9,11},{10,... | collective-permute-start | bytes 12296 | tf_op jit(solution)/shard_map/ppermute | solution.py:309
  31.2 11.0 %all-to-all-start.1 = ((f32[8,2,16,128]{3,2,1,0:T(8,128)}), f32[8,2,16,128]{3,2,1,0:T(8,128)S(1)}, u32[]{:S(2)}, u32[]{:S(2)}) async-start(f32[8,2,16,128]{3,2,1,0:T(8,128)} %bitcast.8), calls=%async_computation.1 | async-start | bytes 262144 | tf_op jit(solution)/shard_map/all_to_all | solution.py:300
  35.6 3.7 %collective-permute-start.6 = (f32[8,128]{1,0:T(8,128)S(1)}, f32[8,128]{1,0:T(8,128)S(1)}, u32[]{:S(2)}, u32[]{:S(2)}) collective-permute-start(f32[8,128]{1,0:T(8,128)S(1)} %add.16), channel_id=1, source_target_pairs={{0,12},{1,13},{2,14},{3,15},{4,8},{5,9},{6,10},{7,11},{8,4},{9,5},... | collective-permute-start | bytes 12296 | tf_op jit(solution)/shard_map/ppermute | solution.py:309
